TPU v7x, 512 devices: a whole 4x4x16 slice. The times are simulated.
512 devices in a mesh: section: 2 (over y_hi), dp: 32 (over y_lo, z), mp: 8 (over x, core).
Axes of the slice: x: 4, y: 4 (y_hi: 2, y_lo: 2; y = y_hi * 2 + y_lo), z: 16, core: 2. Of those that a mesh axis runs over, the one named last changes fastest.
Arguments:
- layer_rows: bfloat16 [2, 8192, 4096], P('section', 'dp'), may hold values from -6 to 6
- cotangent: bfloat16 [8192, 4096], P('dp', 'mp'), may hold values from -6 to 6
- norm_gains: float32 [2, 4096], P('section'), may hold values from 0.5 to 1.5
- projections: bfloat16 [2, 4096, 2, 2048], P('section', 'dp', None, 'mp'), may hold values from -0.09375 to 0.09375
- enc_len: int32 [256], replicated, may hold values from 1 to 64, as said below
- dec_len: int32 [256], replicated, may hold values from 1 to 64, as said below
- enc_dev: int32 [256], replicated, may hold values from 0 to 31, as said below
- dec_dev: int32 [256], replicated, may hold values from 0 to 31, as said below
Outputs:
- grad_rows: bfloat16 [2, 8192, 4096], P('section', 'dp', 'mp')
Inputs may be any that keep to these rules, and one draw needn't show every extreme that they name: The 8 examples of one encoder device (equal enc_dev) have enc_len summing to exactly 256; in every draw some example has exactly 64. The 8 examples of one decoder device (equal dec_dev) have dec_len summing to exactly 256; in every draw some example has exactly 64. Each device number is the enc_dev of exactly 8 examples. Each device number is the dec_dev of exactly 8 examples; the examples of one encoder device have different dec_dev, and those of one decoder device have different enc_dev.
All inputs are finite; a program needn't handle non-finite values.
Results may differ from a plain program's by a relative error of at most 0.022.
Values may be sent and summed in bfloat16 or wider, within the bound.
A program may use at most 64 MiB of HBM per device.

v0:
```python
import jax
import jax.numpy as jnp
from jax import lax
from jax.sharding import PartitionSpec as P

D = 4096
HEAD = 64
EX_DEV = 8


norm_eps = 1e-06


def shifted(block, axis, distance):
    devices = range(lax.axis_size(axis))
    route = [(i - distance, i) for i in devices if i - distance in devices]
    return lax.ppermute(block, axis, route)


def normalize(stream, gain_row):
    values = stream.astype(jnp.float32)
    inverse = lax.rsqrt(jnp.mean(values * values, axis=1, keepdims=True) + norm_eps)
    return ((values * inverse * gain_row[None, :]).astype(jnp.bfloat16), inverse)


def own_examples(dev_table, me_index, ex_count):
    example_total = dev_table.shape[0]
    identity = jnp.arange(example_total, dtype=jnp.int32)
    sort_keys = jnp.where(dev_table == me_index, identity, example_total + identity)
    return jnp.argsort(sort_keys)[:ex_count]


def slot_layout(len_table, dev_table, peer_table, me_index, peer_total, ex_count):
    own_ids = own_examples(dev_table, me_index, ex_count)
    lengths = len_table[own_ids]
    starts = jnp.cumsum(lengths) - lengths
    peer_ids = peer_table[own_ids]
    matches = (peer_ids[None, :] == jnp.arange(peer_total, dtype=jnp.int32)[:, None]).astype(
        jnp.int32
    )
    slot_start = jnp.sum(matches * starts[None, :], axis=1)
    slot_len = jnp.sum(matches * lengths[None, :], axis=1)
    return (slot_start, slot_len)


def row_peers(len_table, dev_table, peer_table, me_index, ex_count, row_count):
    own_ids = own_examples(dev_table, me_index, ex_count)
    lengths = len_table[own_ids]
    starts = jnp.cumsum(lengths) - lengths
    peer_ids = peer_table[own_ids]
    row_ids = jnp.arange(row_count, dtype=jnp.int32)
    local_idx = jnp.sum((row_ids[:, None] >= starts[None, 1:]).astype(jnp.int32), axis=1)
    choose = (local_idx[:, None] == jnp.arange(ex_count, dtype=jnp.int32)[None, :]).astype(
        jnp.int32
    )
    peer_rows = jnp.sum(choose * peer_ids[None, :], axis=1)
    offset_rows = row_ids - jnp.sum(choose * starts[None, :], axis=1)
    return (peer_rows, offset_rows, local_idx)


def to_slots(packed, slot_start, slot_len, slot_depth):
    row_count = packed.shape[0]
    offsets = jnp.arange(slot_depth, dtype=jnp.int32)
    slot_pos = slot_start[:, None] + offsets[None, :]
    live = offsets[None, :] < slot_len[:, None]
    gathered = packed[jnp.clip(slot_pos, 0, row_count - 1)]
    return jnp.where(live[:, :, None, None], gathered, jnp.zeros_like(gathered))


def from_slots(slot_buffer, peer_rows, offset_rows):
    peer_total, slot_depth = (slot_buffer.shape[0], slot_buffer.shape[1])
    flat_slots = slot_buffer.reshape(
        peer_total * slot_depth, slot_buffer.shape[2], slot_buffer.shape[3]
    )
    return flat_slots[peer_rows * slot_depth + offset_rows]


def expand_slots(compact, source_ids, peer_total):
    picker = (source_ids[:, None] == jnp.arange(peer_total, dtype=jnp.int32)[None, :]).astype(
        jnp.bfloat16
    )
    spread = jnp.einsum("ep,eskc->pskc", picker, compact, preferred_element_type=jnp.float32)
    return spread.astype(jnp.bfloat16)


def attend(arrived, queries, grad_out, local_rows, key_lens):
    slot_count, slot_depth = (arrived.shape[0], arrived.shape[1])
    row_count, head_cols = queries.shape
    head_count = head_cols // HEAD
    scale_factor = 1.0 / float(HEAD) ** 0.5
    key_total = slot_count * slot_depth
    flat_kv = arrived.reshape(key_total, 2, head_count, HEAD)
    key_heads = flat_kv[:, 0]
    value_heads = flat_kv[:, 1]
    query_heads = queries.reshape(row_count, head_count, HEAD)
    dout_heads = grad_out.reshape(row_count, head_count, HEAD)
    offsets = jnp.arange(slot_depth, dtype=jnp.int32)
    key_live = (offsets[None, :] < key_lens[:, None]).reshape(key_total)
    key_slot = jnp.arange(key_total, dtype=jnp.int32) // slot_depth
    key_mask = (local_rows[:, None] == key_slot[None, :]) & key_live[None, :]
    scores = (
        jnp.einsum("thc,khc->htk", query_heads, key_heads, preferred_element_type=jnp.float32)
        * scale_factor
    )
    exp_scores = jnp.where(key_mask[None, :, :], jnp.exp(scores), 0.0)
    probs = exp_scores / jnp.sum(exp_scores, axis=2, keepdims=True)
    probs_bf = probs.astype(jnp.bfloat16)
    attended = jnp.einsum(
        "htk,khc->thc", probs_bf, value_heads, preferred_element_type=jnp.float32
    ).astype(jnp.bfloat16)
    grad_probs = jnp.einsum(
        "thc,khc->htk", dout_heads, value_heads, preferred_element_type=jnp.float32
    )
    row_delta = jnp.sum(dout_heads.astype(jnp.float32) * attended.astype(jnp.float32), axis=2).T[
        :, :, None
    ]
    grad_scores = (probs * (grad_probs - row_delta) * scale_factor).astype(jnp.bfloat16)
    grad_query = jnp.einsum(
        "htk,khc->thc", grad_scores, key_heads, preferred_element_type=jnp.float32
    )
    grad_query = grad_query.astype(jnp.bfloat16).reshape(row_count, head_cols)
    grad_keys = jnp.einsum(
        "htk,thc->khc", grad_scores, query_heads, preferred_element_type=jnp.float32
    ).astype(jnp.bfloat16)
    grad_values = jnp.einsum(
        "htk,thc->khc", probs_bf, dout_heads, preferred_element_type=jnp.float32
    ).astype(jnp.bfloat16)
    grad_slots = jnp.stack([grad_keys, grad_values], axis=1).reshape(
        slot_count, slot_depth, 2, head_cols
    )
    return (grad_query, grad_slots)


def shards(layer_rows, cotangent, norm_gains, projections, enc_len, dec_len, enc_dev, dec_dev):
    section_index = lax.axis_index("section")
    device = lax.axis_index("dp")
    mp_index = lax.axis_index("mp")
    peer_total = lax.axis_size("dp")
    ex_count = EX_DEV
    stream = layer_rows[0]
    gain_row = norm_gains[0]
    weight_block = projections[0]
    row_count = stream.shape[0]
    slot_depth = 2 * row_count // ex_count
    normed, inverse = normalize(stream, gain_row)
    full_cot = lax.all_gather(cotangent, "mp", axis=1, tiled=True)
    second_left = jnp.where(section_index == 1, full_cot, normed)
    weight_piece = lax.all_gather(weight_block, "dp", axis=0, tiled=True)
    first_out = jnp.dot(normed, weight_piece[:, 0, :], preferred_element_type=jnp.float32)
    second_out = jnp.dot(second_left, weight_piece[:, 1, :], preferred_element_type=jnp.float32)
    first_out = first_out.astype(jnp.bfloat16)
    second_out = second_out.astype(jnp.bfloat16)
    packed = jnp.stack([first_out, second_out], axis=1)
    enc_slot_start, enc_slot_len = slot_layout(
        enc_len, enc_dev, dec_dev, device, peer_total, ex_count
    )
    enc_peer_rows, enc_offset_rows, unused_local = row_peers(
        enc_len, enc_dev, dec_dev, device, ex_count, row_count
    )
    dec_own = own_examples(dec_dev, device, ex_count)
    source_ids = enc_dev[dec_own]
    key_lens = enc_len[dec_own]
    slot_buffer = to_slots(packed, enc_slot_start, enc_slot_len, slot_depth)
    routed = lax.all_to_all(slot_buffer, "dp", split_axis=0, concat_axis=0, tiled=True)
    arrived = shifted(routed[source_ids], "section", 1)
    query_peers, query_offsets, query_local = row_peers(
        dec_len, dec_dev, enc_dev, device, ex_count, row_count
    )

    def attend_now():
        return attend(arrived, first_out, second_out, query_local, key_lens)

    def skip_now():
        return (jnp.zeros_like(first_out), jnp.zeros_like(arrived))

    grad_query, grad_slots = lax.cond(section_index == 1, attend_now, skip_now)
    crossed_slots = shifted(grad_slots, "section", -1)
    spread_slots = expand_slots(crossed_slots, source_ids, peer_total)
    back_slots = lax.all_to_all(spread_slots, "dp", split_axis=0, concat_axis=0, tiled=True)
    returned = from_slots(back_slots, enc_peer_rows, enc_offset_rows)
    first_grad = returned[:, 0, :] + grad_query
    second_grad = returned[:, 1, :]
    weight_piece = lax.all_gather(weight_block, "dp", axis=0, tiled=True)
    part_one = jnp.einsum(
        "rc,dc->rd", first_grad, weight_piece[:, 0, :], preferred_element_type=jnp.float32
    )
    part_two = jnp.einsum(
        "rc,dc->rd", second_grad, weight_piece[:, 1, :], preferred_element_type=jnp.float32
    )
    row_term = part_one + part_two
    grad_normed = lax.psum_scatter(
        row_term.astype(jnp.bfloat16), "mp", scatter_dimension=1, tiled=True
    ).astype(jnp.float32)
    local_cols = grad_normed.shape[1]
    local_rows = lax.dynamic_slice_in_dim(stream, mp_index * local_cols, local_cols, 1).astype(
        jnp.float32
    )
    local_gain = lax.dynamic_slice_in_dim(gain_row, mp_index * local_cols, local_cols, 0)
    weighted = grad_normed * local_gain[None, :]
    row_stat = lax.psum(jnp.sum(weighted * local_rows, axis=1), "mp")
    result = inverse * weighted - local_rows * inverse**3 * row_stat[:, None] / D
    return result.astype(jnp.bfloat16)[None]


def solution(mesh):
    placed = (
        P("section", "dp", None),
        P("dp", "mp"),
        P("section", None),
        P("section", "dp", None, "mp"),
        P(),
        P(),
        P(),
        P(),
    )
    return jax.shard_map(
        shards, mesh=mesh, in_specs=placed, out_specs=P("section", "dp", "mp"), check_vma=False
    )
```

profile of v0, /device:TPU:1, one launch (start us, length us, event | category | flops | bytes accessed | tf_op | source)
XLA Modules:
  0.0 520.3 jit_solution(10795119498719082610)
XLA Ops:
  6.5 1.7 copy.43
  8.3 0.7 all-gather.4.cloned.1.call-update
  9.1 0.7 compare_select_fusion.5
  9.8 3.1 sort.36
  12.9 1.3 gather_fusion.3
  14.2 1.3 gather_fusion.4
  16.0 2.1 fusion.19
  18.2 116.0 %all-gather.6.cloned.1.call-done = bf16[1,4096,2,256]{3,1,2,0:T(8,128)(2,1)} async-done(((bf16[1,128,2,256]{3,1,2,0:T(8,128)(2,1)}), bf16[1,4096,2,256]{3,1,2,0:T(8,128)(2,1)}) %all-gather.6.cloned.1.call-update) | async-done | bytes 4194320 | tf_op jit(solution)/shard_map/all_gather | solution.py:148
  134.2 2.4 fusion.39
  136.6 45.0 %all-gather.4.cloned.1.call-done = bf16[256,4096]{1,0:T(8,128)(2,1)} async-done(((bf16[256,512]{1,0:T(8,128)(2,1)}), bf16[256,4096]{1,0:T(8,128)(2,1)}) %all-gather.4.cloned.1.call-update) | async-done | bytes 2097168 | tf_op jit(solution)/shard_map/all_gather | solution.py:146
  181.6 2.7 fusion.36
  184.6 7.9 %gather_fusion.5 = bf16[2048,2,256]{2,1,0:T(2,128)(2,1)S(1)} fusion(bf16[256,2,256]{2,1,0:T(2,128)(2,1)S(1)} %copy.44, s32[2048]{0:T(1024)S(1)} %broadcast_clamp_fusion), kind=kCustom, calls=%fused_computation.5 | custom fusion | bytes 4202496 | tf_op jit(solution)/shard_map/gather | solution.py:66
  192.6 1.6 copy_select_fusion
  194.1 13.4 %all-to-all-start = ((bf16[32,64,2,256]{3,1,2,0:T(8,128)(2,1)}), bf16[32,64,2,256]{3,1,2,0:T(8,128)(2,1)S(1)}, u32[]{:S(2)}, u32[]{:S(2)}) async-start(bf16[32,64,2,256]{3,1,2,0:T(8,128)(2,1)} %copy_select_fusion), calls=%async_computation | async-start | bytes 4194304 | tf_op jit(solution)/shard_map/all_to_all | solution.py:164
  207.5 3.1 sort.35
  212.2 87.4 %all-to-all-done = bf16[32,64,2,256]{3,1,2,0:T(8,128)(2,1)S(1)} async-done(((bf16[32,64,2,256]{3,1,2,0:T(8,128)(2,1)}), bf16[32,64,2,256]{3,1,2,0:T(8,128)(2,1)S(1)}, u32[]{:S(2)}, u32[]{:S(2)}) %all-to-all-start) | async-done | bytes 2097184 | tf_op jit(solution)/shard_map/all_to_all | solution.py:164
  300.2 5.0 collective-permute-start
  305.3 7.5 %collective-permute-done = bf16[8,64,2,256]{3,1,2,0:T(8,128)(2,1)S(1)} collective-permute-done((bf16[8,64,2,256]{3,1,2,0:T(8,128)(2,1)S(1)}, bf16[8,64,2,256]{3,1,2,0:T(8,128)(2,1)S(1)}, u32[]{:S(2)}, u32[]{:S(2)}) %collective-permute-start) | collective-permute-done | bytes 524320 | tf_op jit(solution)/shard_map/ppermute | solution.py:17
  313.0 1.2 copy.49
  314.2 1.5 collective-permute-start.1
  315.7 22.7 %collective-permute-done.1 = bf16[8,64,2,256]{3,0,2,1:T(8,128)(2,1)S(1)} collective-permute-done((bf16[8,64,2,256]{3,0,2,1:T(8,128)(2,1)S(1)}, bf16[8,64,2,256]{3,0,2,1:T(8,128)(2,1)S(1)}, u32[]{:S(2)}, u32[]{:S(2)}) %collective-permute-start.1) | collective-permute-done | bytes 524320 | tf_op jit(solution)/shard_map/ppermute | solution.py:17
  338.4 0.8 convolution_convert_fusion.4
  339.2 3.5 copy.50
  342.7 18.0 %all-to-all-start.1 = ((bf16[32,64,2,256]{3,2,1,0:T(2,128)(2,1)}), bf16[32,64,2,256]{3,2,1,0:T(2,128)(2,1)S(1)}, u32[]{:S(2)}, u32[]{:S(2)}) async-start(bf16[32,64,2,256]{3,2,1,0:T(2,128)(2,1)} %copy.50), calls=%async_computation.1 | async-start | bytes 4194304 | tf_op jit(solution)/shard_map/all_to_all | solution.py:179
  361.1 90.7 %all-to-all-done.1 = bf16[32,64,2,256]{3,2,1,0:T(2,128)(2,1)S(1)} async-done(((bf16[32,64,2,256]{3,2,1,0:T(2,128)(2,1)}), bf16[32,64,2,256]{3,2,1,0:T(2,128)(2,1)S(1)}, u32[]{:S(2)}, u32[]{:S(2)}) %all-to-all-start.1) | async-done | bytes 2097184 | tf_op jit(solution)/shard_map/all_to_all | solution.py:179
  451.8 1.2 gather_fusion.7
  453.4 2.5 fusion.35
  456.2 2.1 fusion.18
  458.4 38.0 %reduce-scatter.2.cloned.1.call-done = bf16[256,512]{1,0:T(8,128)(2,1)} async-done(((bf16[256,4096]{1,0:T(8,128)(2,1)}), bf16[256,512]{1,0:T(8,128)(2,1)}) %reduce-scatter.2.cloned.1.call-update) | async-done | bytes 262160 | tf_op jit(solution)/shard_map/reduce_scatter | solution.py:191
  496.4 1.2 fusion.46
  497.6 14.3 %psum.7 = f32[256]{0:T(256)S(1)} all-reduce(f32[256]{0:T(256)S(1)} %fusion.46), channel_id=1, replica_groups=mesh['section'=2,'dp'=32,'mp'=8] {'mp'}, use_global_device_ids=true, to_apply=%region_17.18 | all-reduce | flops 256 | bytes 2048 | tf_op jit(solution)/shard_map/psum | solution.py:200
  511.9 1.9 fusion.47
  (58 shorter events, 4.5 us)
Async XLA Ops:
  6.5 204.8 %copy-start = (s32[256]{0:T(256)S(1)}, s32[256]{0:T(256)}, u32[]{:S(2)}) copy-start(s32[256]{0:T(256)} %param.15) | copy-start | bytes 3076
  6.5 127.6 %copy-start.4 = (bf16[1,256,4096]{2,1,0:T(8,128)(2,1)S(1)}, bf16[1,256,4096]{2,1,0:T(8,128)(2,1)}, u32[]{:S(2)}) copy-start(bf16[1,256,4096]{2,1,0:T(8,128)(2,1)} %param.10) | copy-start | bytes 6291460
  6.5 127.6 %copy-start.7 = (f32[1,4096]{1,0:T(1,128)S(1)}, f32[1,4096]{1,0:T(1,128)}, u32[]{:S(2)}) copy-start(f32[1,4096]{1,0:T(1,128)} %param.12) | copy-start | bytes 49156
  6.5 127.6 %all-gather.6.cloned.1.call-start = ((), (), s32[]{:S(2)}) async-start(), calls=%async_computation.5 | async-start | bytes 4325376 | tf_op jit(solution)/shard_map/all_gather | solution.py:148
  8.3 173.3 %all-gather.4.cloned.1.call-start = ((), (), s32[]{:S(2)}) async-start(), calls=%async_computation.3 | async-start | bytes 2359296 | tf_op jit(solution)/shard_map/all_gather | solution.py:146
  136.6 47.8 %copy-start.5 = (bf16[256,256]{1,0:T(8,128)(2,1)}, bf16[256,256]{1,0:T(8,128)(2,1)S(1)}, u32[]{:S(2)}) copy-start(bf16[256,256]{1,0:T(8,128)(2,1)S(1)} %fusion.39) | copy-start | bytes 393220
  194.1 16.5 %copy-start.2 = (s32[256]{0:T(256)S(1)}, s32[256]{0:T(256)}, u32[]{:S(2)}) copy-start(s32[256]{0:T(256)} %param.16) | copy-start | bytes 3076
  194.1 105.5 %all-to-all-start = ((bf16[32,64,2,256]{3,1,2,0:T(8,128)(2,1)}), bf16[32,64,2,256]{3,1,2,0:T(8,128)(2,1)S(1)}, u32[]{:S(2)}, u32[]{:S(2)}) async-start(bf16[32,64,2,256]{3,1,2,0:T(8,128)(2,1)} %copy_select_fusion), calls=%async_computation | async-start | bytes 4194304 | tf_op jit(solution)/shard_map/all_to_all | solution.py:164
  207.5 105.3 %copy-start.1 = (s32[256]{0:T(256)S(1)}, s32[256]{0:T(256)}, u32[]{:S(2)}) copy-start(s32[256]{0:T(256)} %param.14) | copy-start | bytes 3076
  207.5 105.3 %copy-start.6 = (bf16[256,256]{1,0:T(8,128)(2,1)S(1)}, bf16[256,256]{1,0:T(8,128)(2,1)}, u32[]{:S(2)}) copy-start(bf16[256,256]{1,0:T(8,128)(2,1)} %copy-done.5) | copy-start | bytes 393220
  300.2 12.6 %collective-permute-start = (bf16[8,64,2,256]{3,1,2,0:T(8,128)(2,1)S(1)}, bf16[8,64,2,256]{3,1,2,0:T(8,128)(2,1)S(1)}, u32[]{:S(2)}, u32[]{:S(2)}) collective-permute-start(bf16[8,64,2,256]{3,1,2,0:T(8,128)(2,1)S(1)} %gather_fusion.6), channel_id=1, source_target_pairs={{0,256},{1,257},{2,258},{3,259},{4,260},{5,261},{6,262},{7,263},{8... | collective-permute-start | bytes 1572872 | tf_op jit(solution)/shard_map/ppermute | solution.py:17
  314.2 24.2 %collective-permute-start.1 = (bf16[8,64,2,256]{3,0,2,1:T(8,128)(2,1)S(1)}, bf16[8,64,2,256]{3,0,2,1:T(8,128)(2,1)S(1)}, u32[]{:S(2)}, u32[]{:S(2)}) collective-permute-start(bf16[8,64,2,256]{3,0,2,1:T(8,128)(2,1)S(1)} %copy.49), channel_id=1, source_target_pairs={{256,0},{257,1},{258,2},{259,3},{260,4},{261,5},{262,6},{263,7},{2... | collective-permute-start | bytes 1572872 | tf_op jit(solution)/shard_map/ppermute | solution.py:17
  342.7 109.1 %all-to-all-start.1 = ((bf16[32,64,2,256]{3,2,1,0:T(2,128)(2,1)}), bf16[32,64,2,256]{3,2,1,0:T(2,128)(2,1)S(1)}, u32[]{:S(2)}, u32[]{:S(2)}) async-start(bf16[32,64,2,256]{3,2,1,0:T(2,128)(2,1)} %copy.50), calls=%async_computation.1 | async-start | bytes 4194304 | tf_op jit(solution)/shard_map/all_to_all | solution.py:179
  360.8 135.7 %reduce-scatter.2.cloned.1.call-start = ((), (), s32[]{:S(2)}) async-start(), calls=%async_computation.4 | async-start | bytes 2359296 | tf_op jit(solution)/shard_map/reduce_scatter | solution.py:191
  453.4 2.8 copy-start.3
Sparse Core Ops, SparseCore 0:
  9.4 124.6 all-gather.5
  136.3 45.2 all-gather.3
  458.5 37.8 reduce-scatter.1
where the time goes:
time: 521 us; the launch traced here: 520 us
  waiting for transfers between devices  408 us (78%)
  starting transfers between devices  37.9 us (7%)
  local copies, waits for them, and re-layouts  21.5 us (4%)
  other arithmetic  14.7 us (3%)
  blocking collectives  14.3 us (3%)
  between operations  13.3 us (3%)
  matrix products  10.5 us (2%)
    all_gather x1, waiting for transfers between devices, shards(): weight_piece = lax.all_gather(weight_block, 'dp', axis=0, tiled=True)  116 us
    all_to_all x1, waiting for transfers between devices, shards(): lax.all_to_all(spread_slots, 'dp', split_axis=0, concat_axis=0, tiled=True)  90.7 us
    all_to_all x1, waiting for transfers between devices, shards(): lax.all_to_all(slot_buffer, 'dp', split_axis=0, concat_axis=0, tiled=True)  87.4 us
    all_gather x1, waiting for transfers between devices, shards(): full_cot = lax.all_gather(cotangent, 'mp', axis=1, tiled=True)  45 us
    reduce_scatter x1, waiting for transfers between devices, shards(): lax.psum_scatter(row_term.astype(jnp.bfloat16), 'mp', scatter_dimension=1...  38 us
    ppermute x2, waiting for transfers between devices, shifted(): return lax.ppermute(block, axis, route)  30.2 us
    all_to_all x1, starting transfers between devices, shards(): lax.all_to_all(spread_slots, 'dp', split_axis=0, concat_axis=0, tiled=True)  18 us
    psum x1, blocking collectives, shards(): row_stat = lax.psum(jnp.sum(weighted * local_rows, axis=1), 'mp')  14.3 us
  transfers between devices with their start and end apart: 7, of which 7 were waited for; matrix products, arithmetic and copies ran while one was open for 3% of the time, Pallas kernels for 0%

commit v1 on v0

v1 whole, which is shorter than its diff:
```python
import functools

import jax
import jax.numpy as jnp
from jax import lax
from jax.experimental import pallas as pl
from jax.experimental.pallas import tpu as pltpu
from jax.sharding import PartitionSpec as P

HEAD = 64
EX_DEV = 8
EPS = 1e-06
LANES = 128
CUT = 48
MESH = pl.DeviceIdType.MESH
F32 = jnp.float32
BF16 = jnp.bfloat16


def nt(a, b):
    return lax.dot_general(a, b, (((1,), (1,)), ((), ())), preferred_element_type=F32)


def tn(a, b):
    return lax.dot_general(a, b, (((0,), (0,)), ((), ())), preferred_element_type=F32)


def nn(a, b):
    return jnp.dot(a, b, preferred_element_type=F32)


def kernel(
    n_dp,
    n_mp,
    x_ref,
    gain_ref,
    w_ref,
    cot_ref,
    tab_r,
    tab_c,
    out_ref,
    wall,
    left0,
    left1,
    inv_ref,
    acc,
    qkv,
    grad,
    fidx_ref,
    ridx_ref,
    rank_ref,
    wide,
    send1,
    in1,
    send2,
    in2,
    send3,
    in3,
    send4,
    in4,
    sib_send,
    sib_recv,
    x_send,
    x_recv,
    z_sems,
    y_sems,
    cot_sems,
    w_send_sem,
    cot_send_sem,
    hop_send,
    hop_recv,
    hop_local,
    c_send,
    c_sib,
    c_x,
):
    nz = n_dp // 2
    nx = n_mp // 2
    half = nz // 2
    slots = 2 * n_dp
    rows, features = x_ref.shape
    depth = w_ref.shape[0]
    keep = rows // slots
    section = lax.axis_index("section")
    dp = lax.axis_index("dp")
    mp = lax.axis_index("mp")
    yl = dp // nz
    z = dp % nz
    xx = mp // 2
    core = mp % 2
    me = section * n_dp + dp
    encoder = section == 0
    decoder = section == 1

    barrier = pltpu.get_barrier_semaphore()

    def greet(j, carry):
        peer = (me + j) % slots
        pl.semaphore_signal(
            barrier, inc=1, device_id=(peer // n_dp, peer % n_dp, mp), device_id_type=MESH
        )
        return carry

    def greet_mp(j, carry):
        pl.semaphore_signal(
            barrier, inc=1, device_id=(section, dp, (mp + j) % n_mp), device_id_type=MESH
        )
        return carry

    lax.fori_loop(1, slots, greet, 0)
    lax.fori_loop(1, n_mp, greet_mp, 0)
    pl.semaphore_wait(barrier, slots - 1 + n_mp - 1)

    spans = {"b": (CUT, depth - CUT), "a": (0, CUT), "o": (0, CUT)}
    order = ("b", "a", "o")

    def span(kind, y, zb):
        first, size = spans[kind]
        return wall.at[pl.ds(pl.multiple_of((y * nz + zb) * depth + first, 16), size), :]

    def exists(sign, kind, hop):
        if hop < half:
            return True
        return hop == half and ((kind == "b") == (sign == 1))

    def z_copy(sign, kind, hop, sending):
        y = 1 - yl if kind == "o" else yl
        back = hop - 1 if sending else hop
        part = span(kind, y, (z - sign * back + nz) % nz)
        return pltpu.make_async_remote_copy(
            src_ref=part,
            dst_ref=part,
            send_sem=w_send_sem,
            recv_sem=z_sems.at[(1 - sign) // 2, order.index(kind), hop - 1],
            device_id=(section, yl * nz + (z + sign + nz) % nz, mp),
            device_id_type=MESH,
        )

    def y_slot(sign, hop):
        if hop == 0:
            return 0
        return hop if sign == 1 else half + hop

    def y_copy(kind, sign, hop, sending):
        y = yl if sending else 1 - yl
        part = span(kind, y, (z - sign * hop + nz) % nz)
        slot = nz if kind == "a" else y_slot(sign, hop)
        return pltpu.make_async_remote_copy(
            src_ref=part,
            dst_ref=part,
            send_sem=w_send_sem,
            recv_sem=y_sems.at[slot],
            device_id=(section, (1 - yl) * nz + z, mp),
            device_id_type=MESH,
        )

    wall[pl.ds(pl.multiple_of(dp * depth, depth), depth), :] = w_ref[...]
    for kind in ("b", "a"):
        for sign in (1, -1):
            if exists(sign, kind, 1):
                z_copy(sign, kind, 1, True).start()
        y_copy("a" if kind == "b" else "b", 1, 0, True).start()

    per_mp = features // n_mp // LANES

    def cot_copy(owner, slot, target):
        part = left1.at[pl.ds(owner * per_mp, per_mp)]
        return pltpu.make_async_remote_copy(
            src_ref=part,
            dst_ref=part,
            send_sem=cot_send_sem,
            recv_sem=cot_sems.at[slot],
            device_id=(section, dp, target),
            device_id_type=MESH,
        )

    sibling = xx * 2 + 1 - core

    @pl.when(decoder)
    def _():
        for c in range(per_mp):
            left1[mp * per_mp + c] = cot_ref[:, c * LANES : (c + 1) * LANES]
        for o in (2, 1, 3):
            if o < nx:
                cot_copy(mp, o, (xx + o) % nx * 2 + core).start()
        cot_copy(mp, nx, sibling).start()

    y_copy("a", 1, 0, False).wait_recv()
    for sign in (1, -1):
        if exists(sign, "o", 1):
            z_copy(sign, "o", 1, True).start()

    step = 32 if rows % 32 == 0 else rows

    def norm_rows(i, carry):
        at = pl.ds(pl.multiple_of(i * step, step), step)
        values = x_ref[at, :].astype(F32)
        inverse = lax.rsqrt(jnp.mean(values * values, axis=1, keepdims=True) + EPS)
        inv_ref[at, :] = jnp.broadcast_to(inverse, (step, LANES))
        normed = (values * inverse * gain_ref[...]).astype(BF16)
        for c in range(features // LANES):
            left0[c, at, :] = normed[:, c * LANES : (c + 1) * LANES]

        @pl.when(encoder)
        def _():
            for c in range(features // LANES):
                left1[c, at, :] = normed[:, c * LANES : (c + 1) * LANES]

        return carry

    lax.fori_loop(0, rows // step, norm_rows, 0)

    def tables():
        count = EX_DEV * n_dp
        el_r, dl_r, ed_r, dd_r = (tab_r[k : k + 1, :] for k in range(4))
        el_c, dl_c, ed_c, dd_c = (tab_c[:, k : k + 1] for k in range(4))
        shape = (count, count)
        down = lax.broadcasted_iota(jnp.int32, shape, 0).astype(F32)
        along = lax.broadcasted_iota(jnp.int32, shape, 1).astype(F32)
        zero = jnp.zeros(shape, F32)
        same_enc = ed_r == ed_c
        same_dec = dd_r == dd_c
        dstart_r = jnp.sum(
            jnp.where(same_dec & (down < along), dl_c + zero, 0.0), axis=0, keepdims=True
        )
        rank_r = jnp.sum(jnp.where(same_enc & (down < along), 1.0 + zero, 0.0), axis=0, keepdims=True)
        estart_c = jnp.sum(
            jnp.where(same_enc & (along < down), el_r + zero, 0.0), axis=1, keepdims=True
        )
        rank_c = jnp.sum(jnp.where(same_enc & (along < down), 1.0 + zero, 0.0), axis=1, keepdims=True)
        start_i = dstart_r.astype(jnp.int32)
        offset = (me - start_i) & (slots - 1)
        slot = (start_i + offset) // slots
        source = dd_r * float(4 * keep) + slot.astype(F32)
        value = jnp.where(offset.astype(F32) < dl_r, source + 1.0, 0.0)
        place = ed_r * float(EX_DEV) + rank_r
        fidx = jnp.sum(jnp.where(place == down, value + zero, 0.0), axis=1, keepdims=True) - 1.0
        fidx_ref[...] = jnp.broadcast_to(fidx, fidx_ref.shape)
        q_i = lax.broadcasted_iota(jnp.int32, (n_dp * 2 * keep, count), 0)
        dev_q = (q_i // (2 * keep)).astype(F32)
        side_q = (q_i % (2 * keep) // keep).astype(F32)
        row_q = (q_i % keep * slots + me).astype(F32)
        hit = (dd_r == dev_q) & (dstart_r <= row_q) & (row_q < dstart_r + dl_r)
        target = ed_r * float(2 * EX_DEV) + rank_r + side_q * float(EX_DEV) + 1.0
        ridx = jnp.sum(jnp.where(hit, target, 0.0), axis=1, keepdims=True) - 1.0
        ridx_ref[...] = jnp.broadcast_to(ridx, ridx_ref.shape)
        u_r = lax.broadcasted_iota(jnp.int32, (count, rows), 1).astype(F32)
        mine = (ed_c == dp.astype(F32)) & (estart_c <= u_r) & (u_r < estart_c + el_c)
        rank_u = jnp.sum(jnp.where(mine, rank_c + jnp.zeros_like(u_r), 0.0), axis=0, keepdims=True)
        rank_ref[...] = jnp.broadcast_to(rank_u, rank_ref.shape)

    tables()
    acc[...] = jnp.zeros_like(acc)

    width = w_ref.shape[1] // 2

    def product(blocks):
        total0 = total1 = None
        for y, zb in blocks:
            block = y * nz + zb
            at = pl.ds(pl.multiple_of(block * depth, depth), depth)
            p0 = nn(left0[block], wall[at, :width])
            p1 = nn(left1[block], wall[at, width:])
            total0 = p0 if total0 is None else total0 + p0
            total1 = p1 if total1 is None else total1 + p1
        acc[:, :width] += total0
        acc[:, width:] += total1

    def arrived(hop):
        blocks = []
        for sign in (1, -1):
            if hop == 0 and sign == -1 or hop == half and sign == -1:
                continue
            y_copy("b", sign, hop, False).wait_recv()
            zb = (z - sign * hop + nz) % nz
            blocks += [(yl, zb), (1 - yl, zb)]
        return blocks

    ready = []
    for hop in range(1, half + 1):
        for kind in order:
            for sign in (1, -1):
                if exists(sign, kind, hop):
                    z_copy(sign, kind, hop, False).wait_recv()
                    if exists(sign, kind, hop + 1):
                        z_copy(sign, kind, hop + 1, True).start()
                    if kind == "b":
                        y_copy("b", sign, hop, True).start()
        if hop == max(1, half - 5):

            @pl.when(decoder)
            def _():
                for o in (1, 3, 2):
                    if o < nx:
                        owner = (xx - o + nx) % nx * 2 + core
                        cot_copy(owner, o, sibling).wait_recv()
                        cot_copy(owner, nx + o, sibling).start()

        if hop == max(1, half - 4):

            @pl.when(decoder)
            def _():
                for o in range(nx):
                    owner = (xx - o + nx) % nx * 2 + 1 - core
                    cot_copy(owner, nx + o, sibling).wait_recv()

        ready += [arrived(hop - 1)]
        if hop >= max(1, half - 4):
            for blocks in ready:
                product(blocks)
            ready = []
    product(arrived(half))

    def hop_send_copy(k, src, dst, target_section, target_dp):
        return pltpu.make_async_remote_copy(
            src_ref=src,
            dst_ref=dst,
            send_sem=hop_send.at[k],
            recv_sem=hop_recv.at[k],
            device_id=(target_section, target_dp, mp),
            device_id_type=MESH,
        )

    def block_of(buf, i, size):
        if size is None:
            return buf.at[i]
        return buf.at[pl.ds(pl.multiple_of(i * size, size), size)]

    def wait_bytes(sem, buf, count, size):
        part = buf.at[pl.ds(0, count if size is None else count * size)]
        pltpu.make_async_copy(part, part, sem).wait()

    def spread(k, is_source, src, dst, size=None):
        @pl.when(is_source)
        def _():
            pltpu.make_async_copy(
                block_of(src, me, size), block_of(dst, dp, size), hop_local.at[k]
            ).start()

            def one(j, carry):
                i = (me + j) % slots
                hop_send_copy(
                    k, block_of(src, i, size), block_of(dst, dp, size), i // n_dp, i % n_dp
                ).start()
                return carry

            lax.fori_loop(1, slots, one, 0)
            pltpu.make_async_copy(
                block_of(src, me, size), block_of(dst, dp, size), hop_local.at[k]
            ).wait()
            wait_bytes(hop_recv.at[k], dst, n_dp - 1, size)

        @pl.when(jnp.logical_not(is_source))
        def _():
            wait_bytes(hop_recv.at[k], dst, n_dp, size)

    def collect(k, is_target, target_section, src, dst, size=None):
        def one(j, carry):
            t = (dp + j) % n_dp
            hop_send_copy(
                k, block_of(src, t, size), block_of(dst, me, size), target_section, t
            ).start()
            return carry

        @pl.when(is_target)
        def _():
            pltpu.make_async_copy(
                block_of(src, dp, size), block_of(dst, me, size), hop_local.at[k]
            ).start()

        lax.fori_loop(1, n_dp, one, 0)

        @pl.when(jnp.logical_not(is_target))
        def _():
            one(0, 0)

        @pl.when(is_target)
        def _():
            pltpu.make_async_copy(
                block_of(src, dp, size), block_of(dst, me, size), hop_local.at[k]
            ).wait()
            wait_bytes(hop_recv.at[k], dst, slots - 1, size)

    quarters = 2 * width // LANES
    halves = width // LANES
    qkv[...] = acc[...].astype(BF16)

    @pl.when(decoder)
    def _():
        for b in range(quarters):
            for a in range(keep):
                wide[pl.ds(b * keep + a, slots, stride=quarters * keep), :] = qkv[
                    a * slots : (a + 1) * slots, b * LANES : (b + 1) * LANES
                ].astype(F32)
        send1[...] = wide[...].astype(BF16).reshape(send1.shape)

    spread(0, decoder, send1, in1)

    first_in = in1[...].reshape(n_dp * quarters * keep, LANES)
    span_f = lax.broadcasted_iota(
        jnp.int32, (n_dp * EX_DEV, n_dp * quarters * keep), 1
    ).astype(F32)
    pieces = []
    for b in range(quarters):
        at = jnp.where(fidx_ref[:, :1] >= 0.0, fidx_ref[:, :1] + float(b * keep), -1.0)
        pick = jnp.where(span_f == at, 1.0, 0.0).astype(BF16)
        pieces += [nn(pick, first_in).reshape(n_dp, EX_DEV, LANES)]
    send2[...] = jnp.concatenate(pieces, axis=1).astype(BF16)
    collect(1, encoder, 0, send2, in2)

    @pl.when(encoder)
    def _():
        scale = 1.0 / float(HEAD) ** 0.5
        total = slots * EX_DEV
        incoming = in2[...].astype(F32)
        parts = [
            incoming[:, b * EX_DEV : (b + 1) * EX_DEV, :].reshape(total, LANES).astype(BF16)
            for b in range(quarters)
        ]
        example = (lax.broadcasted_iota(jnp.int32, (total, rows), 0) % EX_DEV).astype(F32)
        mask = example == rank_ref[:1, :]
        back = []
        for b in range(halves):
            both = []
            for s in range(LANES // HEAD):
                low = b * LANES + s * HEAD
                q = parts[b][:, s * HEAD : (s + 1) * HEAD]
                dout = parts[halves + b][:, s * HEAD : (s + 1) * HEAD]
                k = qkv[:, low : low + HEAD]
                v = qkv[:, width + low : width + low + HEAD]
                weight = jnp.where(mask, jnp.exp(nt(q, k) * scale), 0.0)
                probs = weight / jnp.sum(weight, axis=1, keepdims=True)
                probs_bf = probs.astype(BF16)
                attended = nn(probs_bf, v).astype(BF16)
                delta = jnp.sum(
                    dout.astype(F32) * attended.astype(F32), axis=1, keepdims=True
                )
                dscore = (probs * (nt(dout, v) - delta) * scale).astype(BF16)
                both += [nn(dscore, k)]
                grad[:, low : low + HEAD] = tn(dscore, q).astype(BF16)
                grad[:, width + low : width + low + HEAD] = tn(probs_bf, dout).astype(BF16)
            back += [jnp.concatenate(both, axis=1).reshape(slots, EX_DEV, LANES)]
        send3[...] = jnp.concatenate(back, axis=1).astype(BF16)

    spread(2, encoder, send3, in3)
    third_in = in3[...].reshape(n_dp * halves * EX_DEV, LANES)
    span_r = lax.broadcasted_iota(
        jnp.int32, (n_dp * halves * keep, n_dp * halves * EX_DEV), 1
    ).astype(F32)
    pick_r = jnp.where(span_r == ridx_ref[:, :1], 1.0, 0.0).astype(BF16)
    send4[...] = nn(pick_r, third_in)
    collect(3, decoder, 1, send4, in4, halves * keep)

    @pl.when(decoder)
    def _():
        for b in range(halves):
            for a in range(keep):
                grad[a * slots : (a + 1) * slots, b * LANES : (b + 1) * LANES] = in4[
                    pl.ds(b * keep + a, slots, stride=halves * keep), :
                ].astype(BF16)
        grad[:, width:] = jnp.zeros((rows, width), BF16)

    columns = features // n_mp
    share = jnp.sum(grad[...].astype(F32) * qkv[...].astype(F32), axis=1, keepdims=True)
    inverse = inv_ref[:, :1]
    slope = inverse * inverse * share * (1.0 / features)

    def term(owner):
        at = pl.ds(pl.multiple_of(owner * columns, columns), columns)
        raw = nt(grad[...], wall[at, :])
        return inverse * (raw * gain_ref[:, at]) - x_ref[:, at].astype(F32) * slope

    def sib_copy(o):
        return pltpu.make_async_remote_copy(
            src_ref=sib_send.at[o],
            dst_ref=sib_recv.at[o],
            send_sem=c_send.at[0],
            recv_sem=c_sib.at[o],
            device_id=(section, dp, sibling),
            device_id_type=MESH,
        )

    def x_copy(o):
        return pltpu.make_async_remote_copy(
            src_ref=x_send.at[o],
            dst_ref=x_recv.at[o],
            send_sem=c_send.at[1],
            recv_sem=c_x.at[o],
            device_id=(section, dp, (xx + o) % nx * 2 + core),
            device_id_type=MESH,
        )

    def to_sibling(o):
        sib_send[o] = term((xx + o) % nx * 2 + 1 - core).astype(BF16)
        sib_copy(o).start()

    turns = [o for o in (2, 1, 3, 0) if o < nx]
    to_sibling(turns[0])
    for k, o in enumerate(turns):
        if k + 1 < len(turns):
            to_sibling(turns[k + 1])
        own = term((xx + o) % nx * 2 + core)
        sib_copy(o).wait_recv()
        both = own + sib_recv[o].astype(F32)
        if o:
            x_send[o] = both.astype(BF16)
            x_copy(o).start()
        else:
            result = both
    for o in (1, 3, 2):
        if o < nx:
            x_copy(o).wait_recv()
            result = result + x_recv[o].astype(F32)
    out_ref[...] = result.astype(out_ref.dtype)

    for kind in order:
        for sign in (1, -1):
            for hop in range(1, half + 1):
                if exists(sign, kind, hop):
                    z_copy(sign, kind, hop, True).wait_send()
    y_copy("a", 1, 0, True).wait_send()
    for hop in range(half + 1):
        for sign in (1, -1):
            if (hop == 0 or hop == half) and sign == -1:
                continue
            y_copy("b", sign, hop, True).wait_send()

    @pl.when(decoder)
    def _():
        for o in range(1, 2 * nx):
            cot_copy(mp, o, sibling).wait_send()

    def sent(k, buf, count, size=None):
        wait_bytes(hop_send.at[k], buf, count, size)

    @pl.when(decoder)
    def _():
        sent(0, send1, slots - 1)
        sent(1, send2, n_dp)
        sent(3, send4, n_dp - 1, halves * keep)

    @pl.when(encoder)
    def _():
        sent(1, send2, n_dp - 1)
        sent(2, send3, slots - 1)
        sent(3, send4, n_dp, halves * keep)

    for o in range(nx):
        sib_copy(o).wait_send()
        if o:
            x_copy(o).wait_send()


def shards(n_dp, n_mp, layer_rows, cotangent, norm_gains, projections, enc_len, dec_len, enc_dev, dec_dev):
    x = layer_rows[0]
    rows, features = x.shape
    depth, _, width = projections.shape[1:]
    w = projections[0].reshape(depth, 2 * width)
    count = enc_len.shape[0]
    tab_r = jnp.stack([enc_len, dec_len, enc_dev, dec_dev]).astype(F32)
    tab_c = tab_r.T
    slots = 2 * n_dp
    keep = rows // slots
    quarters = 2 * width // LANES
    halves = width // LANES
    nx = n_mp // 2
    nz = n_dp // 2
    columns = features // n_mp
    vmem = pl.BlockSpec(memory_space=pltpu.VMEM)
    dma = pltpu.SemaphoreType.DMA
    out = pl.pallas_call(
        functools.partial(kernel, n_dp, n_mp),
        out_shape=jax.ShapeDtypeStruct((rows, columns), BF16),
        in_specs=[vmem] * 6,
        out_specs=vmem,
        scratch_shapes=[
            pltpu.VMEM((features, 2 * width), BF16),
            pltpu.VMEM((features // LANES, rows, LANES), BF16),
            pltpu.VMEM((features // LANES, rows, LANES), BF16),
            pltpu.VMEM((rows, LANES), F32),
            pltpu.VMEM((rows, 2 * width), F32),
            pltpu.VMEM((rows, 2 * width), BF16),
            pltpu.VMEM((rows, 2 * width), BF16),
            pltpu.VMEM((count, LANES), F32),
            pltpu.VMEM((n_dp * halves * keep, LANES), F32),
            pltpu.VMEM((8, rows), F32),
            pltpu.VMEM((slots * quarters * keep, LANES), F32),
            pltpu.VMEM((slots, quarters * keep, LANES), BF16),
            pltpu.VMEM((n_dp, quarters * keep, LANES), BF16),
            pltpu.VMEM((n_dp, quarters * EX_DEV, LANES), BF16),
            pltpu.VMEM((slots, quarters * EX_DEV, LANES), BF16),
            pltpu.VMEM((slots, halves * EX_DEV, LANES), BF16),
            pltpu.VMEM((n_dp, halves * EX_DEV, LANES), BF16),
            pltpu.VMEM((n_dp * halves * keep, LANES), F32),
            pltpu.VMEM((slots * halves * keep, LANES), F32),
            pltpu.VMEM((nx, rows, columns), BF16),
            pltpu.VMEM((nx, rows, columns), BF16),
            pltpu.VMEM((nx, rows, columns), BF16),
            pltpu.VMEM((nx, rows, columns), BF16),
            dma((2, 3, max(1, nz // 2))),
            dma((nz + 1,)),
            dma((2 * nx,)),
            dma,
            dma,
            dma((4,)),
            dma((4,)),
            dma((4,)),
            dma((2,)),
            dma((nx,)),
            dma((nx,)),
        ],
        compiler_params=pltpu.CompilerParams(
            collective_id=0, has_side_effects=True, vmem_limit_bytes=52 * 2**20
        ),
    )(x, norm_gains, w, cotangent, tab_r, tab_c)
    return out[None]


def solution(mesh):
    placed = (
        P("section", "dp", None),
        P("dp", "mp"),
        P("section", None),
        P("section", "dp", None, "mp"),
        P(),
        P(),
        P(),
        P(),
    )
    return jax.shard_map(
        functools.partial(shards, mesh.shape["dp"], mesh.shape["mp"]),
        mesh=mesh,
        in_specs=placed,
        out_specs=P("section", "dp", "mp"),
        check_vma=False,
    )
```

time: 521 us -> 137 us (0.26)
  the two profiles are of different devices: /device:TPU:1 before, /device:TPU:25 now
where the time goes in v1:
time: 137 us
  Pallas kernels  133 us (97%)
  local copies, waits for them, and re-layouts  3.43 us (3%)
    pallas_call x1, Pallas kernels, shards(): pl.pallas_call(functools.partial(kernel, n_dp, n_mp), out_shape=jax.Shape...  133 us
    unnamed x6, local copies, waits for them, and re-layouts  3.29 us

profile of v1, /device:TPU:25, one launch (start us, length us, event | category | flops | bytes accessed | tf_op | source)
XLA Modules:
  0.0 136.8 jit_solution(8513886326031270098)
XLA Ops:
  0.0 0.7 add_convert_fusion.tab_r
  0.7 0.1 copy.17
  0.9 0.9 copy.18
  1.8 0.0 copy-start
  1.8 0.9 copy-done
  2.8 0.0 copy-start.1
  2.8 0.7 copy-done.1
  3.5 132.6 %shard_map.82 = bf16[256,512]{1,0:T(8,128)(2,1)S(1)} custom-call(bf16[256,4096]{1,0:T(8,128)(2,1)} %bitcast.13, f32[1,4096]{1,0:T(1,128)S(1)} %copy-done.1, bf16[128,512]{1,0:T(8,128)(2,1)S(1)} %bitcast.12, bf16[256,512]{1,0:T(8,128)(2,1)S(1)} %copy-done, f32[4,256]{1,0:T(4,128)S(1)} %add_convert_fusion.tab_r, f32[256,4]{1,0:T(8,128)S(1)} %bitcast.11), custom_call_target="tpu_custom_call" | custom-call | tf_op jit(solution)/shard_map/pallas_call | solution.py:571
  136.1 0.7 copy.20
Async XLA Ops:
  1.8 1.0 copy-start
  2.8 0.7 copy-start.1

commit v2 on v1

--- a/solution.py
+++ b/solution.py
@@ -32,13 +32,19 @@
 def kernel(
     n_dp,
     n_mp,
+    x_hbm,
+    gain_hbm,
+    w_hbm,
+    cot_hbm,
+    el_ref,
+    dl_ref,
+    ed_ref,
+    dd_ref,
+    out_ref,
     x_ref,
     gain_ref,
     w_ref,
     cot_ref,
-    tab_r,
-    tab_c,
-    out_ref,
     wall,
     left0,
     left1,
@@ -46,8 +52,8 @@
     acc,
     qkv,
     grad,
-    fidx_ref,
-    ridx_ref,
+    pick_ref,
+    pick_back,
     rank_ref,
     wide,
     send1,
@@ -62,6 +68,8 @@
     sib_recv,
     x_send,
     x_recv,
+    in_sems,
+    cross_sem,
     z_sems,
     y_sems,
     cot_sems,
@@ -79,8 +87,10 @@
     half = nz // 2
     slots = 2 * n_dp
     rows, features = x_ref.shape
-    depth = w_ref.shape[0]
+    depth, _, width = w_ref.shape
     keep = rows // slots
+    quarters = 2 * width // LANES
+    halves = width // LANES
     section = lax.axis_index("section")
     dp = lax.axis_index("dp")
     mp = lax.axis_index("mp")
@@ -92,24 +102,28 @@
     encoder = section == 0
     decoder = section == 1
 
+    inputs = [
+        pltpu.make_async_copy(source, target, in_sems.at[k])
+        for k, (source, target) in enumerate(
+            ((w_hbm, w_ref), (cot_hbm, cot_ref), (x_hbm, x_ref), (gain_hbm, gain_ref))
+        )
+    ]
+    for copy in inputs:
+        copy.start()
+
+    sibling = xx * 2 + 1 - core
+    across = 1 - section
+    greeted = [(section, yl * nz + (z + 1) % nz, mp), (section, yl * nz + (z + nz - 1) % nz, mp)]
+    greeted += [(section, (1 - yl) * nz + z, mp), (across, dp, mp), (section, dp, sibling)]
+    greeted += [(section, dp, (xx + o) % nx * 2 + core) for o in range(1, nx)]
     barrier = pltpu.get_barrier_semaphore()
-
-    def greet(j, carry):
-        peer = (me + j) % slots
-        pl.semaphore_signal(
-            barrier, inc=1, device_id=(peer // n_dp, peer % n_dp, mp), device_id_type=MESH
-        )
-        return carry
-
-    def greet_mp(j, carry):
-        pl.semaphore_signal(
-            barrier, inc=1, device_id=(section, dp, (mp + j) % n_mp), device_id_type=MESH
-        )
-        return carry
-
-    lax.fori_loop(1, slots, greet, 0)
-    lax.fori_loop(1, n_mp, greet_mp, 0)
-    pl.semaphore_wait(barrier, slots - 1 + n_mp - 1)
+    for target in greeted:
+        pl.semaphore_signal(barrier, inc=1, device_id=target, device_id_type=MESH)
+    inputs[0].wait()
+    own = pl.ds(pl.multiple_of(dp * depth, depth), depth)
+    wall[own, :width] = w_ref[:, 0, :]
+    wall[own, width:] = w_ref[:, 1, :]
+    pl.semaphore_wait(barrier, len(greeted))
 
     spans = {"b": (CUT, depth - CUT), "a": (0, CUT), "o": (0, CUT)}
     order = ("b", "a", "o")
@@ -154,7 +168,6 @@
             device_id_type=MESH,
         )
 
-    wall[pl.ds(pl.multiple_of(dp * depth, depth), depth), :] = w_ref[...]
     for kind in ("b", "a"):
         for sign in (1, -1):
             if exists(sign, kind, 1):
@@ -174,7 +187,7 @@
             device_id_type=MESH,
         )
 
-    sibling = xx * 2 + 1 - core
+    inputs[1].wait()
 
     @pl.when(decoder)
     def _():
@@ -192,8 +205,8 @@
 
     step = 32 if rows % 32 == 0 else rows
 
-    def norm_rows(i, carry):
-        at = pl.ds(pl.multiple_of(i * step, step), step)
+    def norm_rows(i):
+        at = pl.ds(i * step, step)
         values = x_ref[at, :].astype(F32)
         inverse = lax.rsqrt(jnp.mean(values * values, axis=1, keepdims=True) + EPS)
         inv_ref[at, :] = jnp.broadcast_to(inverse, (step, LANES))
@@ -206,58 +219,77 @@
             for c in range(features // LANES):
                 left1[c, at, :] = normed[:, c * LANES : (c + 1) * LANES]
 
-        return carry
-
-    lax.fori_loop(0, rows // step, norm_rows, 0)
-
-    def tables():
-        count = EX_DEV * n_dp
-        el_r, dl_r, ed_r, dd_r = (tab_r[k : k + 1, :] for k in range(4))
-        el_c, dl_c, ed_c, dd_c = (tab_c[:, k : k + 1] for k in range(4))
+    count = EX_DEV * n_dp
+    el_r, dl_r, ed_r, dd_r = (t[...].astype(F32) for t in (el_ref, dl_ref, ed_ref, dd_ref))
+    found = {}
+
+    def starts():
         shape = (count, count)
         down = lax.broadcasted_iota(jnp.int32, shape, 0).astype(F32)
         along = lax.broadcasted_iota(jnp.int32, shape, 1).astype(F32)
-        zero = jnp.zeros(shape, F32)
+
+        def column(row):
+            return jnp.sum(jnp.where(down == along, row, 0.0), axis=1, keepdims=True)
+
+        el_c, dl_c, ed_c, dd_c = (column(t) for t in (el_r, dl_r, ed_r, dd_r))
         same_enc = ed_r == ed_c
         same_dec = dd_r == dd_c
+        one = jnp.ones(shape, F32)
         dstart_r = jnp.sum(
-            jnp.where(same_dec & (down < along), dl_c + zero, 0.0), axis=0, keepdims=True
-        )
-        rank_r = jnp.sum(jnp.where(same_enc & (down < along), 1.0 + zero, 0.0), axis=0, keepdims=True)
+            jnp.where(same_dec & (down < along), dl_c * one, 0.0), axis=0, keepdims=True
+        )
+        rank_r = jnp.sum(jnp.where(same_enc & (down < along), one, 0.0), axis=0, keepdims=True)
         estart_c = jnp.sum(
-            jnp.where(same_enc & (along < down), el_r + zero, 0.0), axis=1, keepdims=True
-        )
-        rank_c = jnp.sum(jnp.where(same_enc & (along < down), 1.0 + zero, 0.0), axis=1, keepdims=True)
-        start_i = dstart_r.astype(jnp.int32)
+            jnp.where(same_enc & (along < down), el_r * one, 0.0), axis=1, keepdims=True
+        )
+        rank_c = jnp.sum(jnp.where(same_enc & (along < down), one, 0.0), axis=1, keepdims=True)
+        found.update(down=down, dstart_r=dstart_r, rank_r=rank_r)
+        u_r = lax.broadcasted_iota(jnp.int32, (count, rows), 1).astype(F32)
+        mine = (ed_c == dp.astype(F32)) & (estart_c <= u_r) & (u_r < estart_c + el_c)
+        rank_u = jnp.sum(jnp.where(mine, rank_c * jnp.ones_like(u_r), 0.0), axis=0, keepdims=True)
+        rank_ref[...] = jnp.broadcast_to(rank_u, rank_ref.shape)
+
+    def pick_rows():
+        start_i = found["dstart_r"].astype(jnp.int32)
         offset = (me - start_i) & (slots - 1)
         slot = (start_i + offset) // slots
-        source = dd_r * float(4 * keep) + slot.astype(F32)
+        source = dd_r * float(quarters * keep) + slot.astype(F32)
         value = jnp.where(offset.astype(F32) < dl_r, source + 1.0, 0.0)
-        place = ed_r * float(EX_DEV) + rank_r
-        fidx = jnp.sum(jnp.where(place == down, value + zero, 0.0), axis=1, keepdims=True) - 1.0
-        fidx_ref[...] = jnp.broadcast_to(fidx, fidx_ref.shape)
-        q_i = lax.broadcasted_iota(jnp.int32, (n_dp * 2 * keep, count), 0)
-        dev_q = (q_i // (2 * keep)).astype(F32)
-        side_q = (q_i % (2 * keep) // keep).astype(F32)
+        place = ed_r * float(EX_DEV) + found["rank_r"]
+        down = found["down"]
+        found["fidx"] = (
+            jnp.sum(jnp.where(place == down, value * jnp.ones_like(down), 0.0), axis=1, keepdims=True)
+            - 1.0
+        )
+
+    def pick_side(b):
+        fidx = found["fidx"]
+        place = lax.broadcasted_iota(
+            jnp.int32, (n_dp * EX_DEV, n_dp * quarters * keep), 1
+        ).astype(F32)
+        at = jnp.where(fidx >= 0.0, fidx + float(b * keep), -1.0)
+        pick_ref[b] = jnp.where(place == at, 1.0, 0.0).astype(BF16)
+
+    def pick_back_rows():
+        q_i = lax.broadcasted_iota(jnp.int32, (n_dp * halves * keep, count), 0)
+        dev_q = (q_i // (halves * keep)).astype(F32)
+        side_q = (q_i % (halves * keep) // keep).astype(F32)
         row_q = (q_i % keep * slots + me).astype(F32)
+        dstart_r = found["dstart_r"]
         hit = (dd_r == dev_q) & (dstart_r <= row_q) & (row_q < dstart_r + dl_r)
-        target = ed_r * float(2 * EX_DEV) + rank_r + side_q * float(EX_DEV) + 1.0
+        target = (
+            ed_r * float(halves * EX_DEV) + found["rank_r"] + side_q * float(EX_DEV) + 1.0
+        )
         ridx = jnp.sum(jnp.where(hit, target, 0.0), axis=1, keepdims=True) - 1.0
-        ridx_ref[...] = jnp.broadcast_to(ridx, ridx_ref.shape)
-        u_r = lax.broadcasted_iota(jnp.int32, (count, rows), 1).astype(F32)
-        mine = (ed_c == dp.astype(F32)) & (estart_c <= u_r) & (u_r < estart_c + el_c)
-        rank_u = jnp.sum(jnp.where(mine, rank_c + jnp.zeros_like(u_r), 0.0), axis=0, keepdims=True)
-        rank_ref[...] = jnp.broadcast_to(rank_u, rank_ref.shape)
-
-    tables()
-    acc[...] = jnp.zeros_like(acc)
-
-    width = w_ref.shape[1] // 2
-
-    def product(blocks):
+        place = lax.broadcasted_iota(
+            jnp.int32, (n_dp * halves * keep, n_dp * halves * EX_DEV), 1
+        ).astype(F32)
+        pick_back[...] = jnp.where(place == ridx, 1.0, 0.0).astype(BF16)
+
+    def product(y, zb):
         total0 = total1 = None
-        for y, zb in blocks:
-            block = y * nz + zb
+        for row in (y, 1 - y):
+            block = row * nz + zb
             at = pl.ds(pl.multiple_of(block * depth, depth), depth)
             p0 = nn(left0[block], wall[at, :width])
             p1 = nn(left1[block], wall[at, width:])
@@ -266,18 +298,39 @@
         acc[:, :width] += total0
         acc[:, width:] += total1
 
-    def arrived(hop):
-        blocks = []
-        for sign in (1, -1):
-            if hop == 0 and sign == -1 or hop == half and sign == -1:
-                continue
-            y_copy("b", sign, hop, False).wait_recv()
-            zb = (z - sign * hop + nz) % nz
-            blocks += [(yl, zb), (1 - yl, zb)]
-        return blocks
-
-    ready = []
+    def arrived(sign, hop):
+        y_copy("b", sign, hop, False).wait_recv()
+        product(yl, (z - sign * hop + nz) % nz)
+
+    def cot_pass(o):
+        @pl.when(decoder)
+        def _():
+            owner = (xx - o + nx) % nx * 2 + core
+            cot_copy(owner, o, sibling).wait_recv()
+            cot_copy(owner, nx + o, sibling).start()
+
+    def cot_wait():
+        @pl.when(decoder)
+        def _():
+            for o in range(nx):
+                owner = (xx - o + nx) % nx * 2 + 1 - core
+                cot_copy(owner, nx + o, sibling).wait_recv()
+
+    def first_norm():
+        inputs[2].wait()
+        inputs[3].wait()
+        norm_rows(0)
+
+    acc[...] = jnp.zeros_like(acc)
+    items = [first_norm] + [functools.partial(norm_rows, i) for i in range(1, rows // step)]
+    items += [starts, pick_rows] + [functools.partial(pick_side, b) for b in range(quarters)]
+    items += [pick_back_rows]
+    late = [functools.partial(cot_pass, o) for o in (1, 3, 2) if o < nx] + [cot_wait]
+    late += [functools.partial(arrived, 1, 0)]
     for hop in range(1, half + 1):
+        if hop == max(1, half - 3):
+            items += late
+            late = []
         for kind in order:
             for sign in (1, -1):
                 if exists(sign, kind, hop):
@@ -286,30 +339,15 @@
                         z_copy(sign, kind, hop + 1, True).start()
                     if kind == "b":
                         y_copy("b", sign, hop, True).start()
-        if hop == max(1, half - 5):
-
-            @pl.when(decoder)
-            def _():
-                for o in (1, 3, 2):
-                    if o < nx:
-                        owner = (xx - o + nx) % nx * 2 + core
-                        cot_copy(owner, o, sibling).wait_recv()
-                        cot_copy(owner, nx + o, sibling).start()
-
-        if hop == max(1, half - 4):
-
-            @pl.when(decoder)
-            def _():
-                for o in range(nx):
-                    owner = (xx - o + nx) % nx * 2 + 1 - core
-                    cot_copy(owner, nx + o, sibling).wait_recv()
-
-        ready += [arrived(hop - 1)]
-        if hop >= max(1, half - 4):
-            for blocks in ready:
-                product(blocks)
-            ready = []
-    product(arrived(half))
+                    if items:
+                        items.pop(0)()
+        for sign in (1, -1) if hop < half else (1,):
+            (late if late else items).append(functools.partial(arrived, sign, hop))
+    for item in items:
+        item()
+
+    pl.semaphore_signal(cross_sem, inc=1, device_id=(across, dp, mp), device_id_type=MESH)
+    pl.semaphore_wait(cross_sem, 1)
 
     def hop_send_copy(k, src, dst, target_section, target_dp):
         return pltpu.make_async_remote_copy(
@@ -337,14 +375,21 @@
                 block_of(src, me, size), block_of(dst, dp, size), hop_local.at[k]
             ).start()
 
-            def one(j, carry):
-                i = (me + j) % slots
-                hop_send_copy(
-                    k, block_of(src, i, size), block_of(dst, dp, size), i // n_dp, i % n_dp
-                ).start()
+            run = 9 if (slots - 1) % 9 == 0 else 1
+
+            def some(g, carry):
+                for r in range(run):
+                    i = (me + 1 + g * run + r) & (slots - 1)
+                    hop_send_copy(
+                        k,
+                        block_of(src, i, size),
+                        block_of(dst, dp, size),
+                        i // n_dp,
+                        i & (n_dp - 1),
+                    ).start()
                 return carry
 
-            lax.fori_loop(1, slots, one, 0)
+            lax.fori_loop(0, (slots - 1) // run, some, 0)
             pltpu.make_async_copy(
                 block_of(src, me, size), block_of(dst, dp, size), hop_local.at[k]
             ).wait()
@@ -355,11 +400,17 @@
             wait_bytes(hop_recv.at[k], dst, n_dp, size)
 
     def collect(k, is_target, target_section, src, dst, size=None):
-        def one(j, carry):
-            t = (dp + j) % n_dp
+        def one(j):
+            t = (dp + j) & (n_dp - 1)
             hop_send_copy(
                 k, block_of(src, t, size), block_of(dst, me, size), target_section, t
             ).start()
+
+        run = 10 if (n_dp - 2) % 10 == 0 else 1
+
+        def some(g, carry):
+            for r in range(run):
+                one(1 + g * run + r)
             return carry
 
         @pl.when(is_target)
@@ -368,11 +419,12 @@
                 block_of(src, dp, size), block_of(dst, me, size), hop_local.at[k]
             ).start()
 
-        lax.fori_loop(1, n_dp, one, 0)
+        lax.fori_loop(0, (n_dp - 2) // run, some, 0)
+        one(n_dp - 1)
 
         @pl.when(jnp.logical_not(is_target))
         def _():
-            one(0, 0)
+            one(0)
 
         @pl.when(is_target)
         def _():
@@ -381,8 +433,6 @@
             ).wait()
             wait_bytes(hop_recv.at[k], dst, slots - 1, size)
 
-    quarters = 2 * width // LANES
-    halves = width // LANES
     qkv[...] = acc[...].astype(BF16)
 
     @pl.when(decoder)
@@ -397,14 +447,7 @@
     spread(0, decoder, send1, in1)
 
     first_in = in1[...].reshape(n_dp * quarters * keep, LANES)
-    span_f = lax.broadcasted_iota(
-        jnp.int32, (n_dp * EX_DEV, n_dp * quarters * keep), 1
-    ).astype(F32)
-    pieces = []
-    for b in range(quarters):
-        at = jnp.where(fidx_ref[:, :1] >= 0.0, fidx_ref[:, :1] + float(b * keep), -1.0)
-        pick = jnp.where(span_f == at, 1.0, 0.0).astype(BF16)
-        pieces += [nn(pick, first_in).reshape(n_dp, EX_DEV, LANES)]
+    pieces = [nn(pick_ref[b], first_in).reshape(n_dp, EX_DEV, LANES) for b in range(quarters)]
     send2[...] = jnp.concatenate(pieces, axis=1).astype(BF16)
     collect(1, encoder, 0, send2, in2)
 
@@ -420,35 +463,34 @@
         example = (lax.broadcasted_iota(jnp.int32, (total, rows), 0) % EX_DEV).astype(F32)
         mask = example == rank_ref[:1, :]
         back = []
+        lane = lax.broadcasted_iota(jnp.int32, (1, LANES), 1) // HEAD
         for b in range(halves):
-            both = []
+            q, dout = parts[b], parts[halves + b]
+            k = qkv[:, b * LANES : (b + 1) * LANES]
+            v = qkv[:, width + b * LANES : width + (b + 1) * LANES]
+            sums = []
             for s in range(LANES // HEAD):
-                low = b * LANES + s * HEAD
-                q = parts[b][:, s * HEAD : (s + 1) * HEAD]
-                dout = parts[halves + b][:, s * HEAD : (s + 1) * HEAD]
-                k = qkv[:, low : low + HEAD]
-                v = qkv[:, width + low : width + low + HEAD]
-                weight = jnp.where(mask, jnp.exp(nt(q, k) * scale), 0.0)
-                probs = weight / jnp.sum(weight, axis=1, keepdims=True)
+                here = lane == s
+                q_s = jnp.where(here, q, jnp.zeros_like(q))
+                dout_s = jnp.where(here, dout, jnp.zeros_like(dout))
+                weight = jnp.where(mask, jnp.exp(nt(q_s, k) * scale), 0.0)
+                probs = weight * (1.0 / jnp.sum(weight, axis=1, keepdims=True))
                 probs_bf = probs.astype(BF16)
                 attended = nn(probs_bf, v).astype(BF16)
                 delta = jnp.sum(
-                    dout.astype(F32) * attended.astype(F32), axis=1, keepdims=True
+                    dout_s.astype(F32) * attended.astype(F32), axis=1, keepdims=True
                 )
-                dscore = (probs * (nt(dout, v) - delta) * scale).astype(BF16)
-                both += [nn(dscore, k)]
-                grad[:, low : low + HEAD] = tn(dscore, q).astype(BF16)
-                grad[:, width + low : width + low + HEAD] = tn(probs_bf, dout).astype(BF16)
-            back += [jnp.concatenate(both, axis=1).reshape(slots, EX_DEV, LANES)]
+                dscore = (probs * (nt(dout_s, v) - delta) * scale).astype(BF16)
+                news = (nn(dscore, k), tn(dscore, q), tn(probs_bf, dout))
+                sums = [jnp.where(here, new, old) for new, old in zip(news, sums)] if s else news
+            grad[:, b * LANES : (b + 1) * LANES] = sums[1].astype(BF16)
+            grad[:, width + b * LANES : width + (b + 1) * LANES] = sums[2].astype(BF16)
+            back += [sums[0].reshape(slots, EX_DEV, LANES)]
         send3[...] = jnp.concatenate(back, axis=1).astype(BF16)
 
     spread(2, encoder, send3, in3)
     third_in = in3[...].reshape(n_dp * halves * EX_DEV, LANES)
-    span_r = lax.broadcasted_iota(
-        jnp.int32, (n_dp * halves * keep, n_dp * halves * EX_DEV), 1
-    ).astype(F32)
-    pick_r = jnp.where(span_r == ridx_ref[:, :1], 1.0, 0.0).astype(BF16)
-    send4[...] = nn(pick_r, third_in)
+    send4[...] = nn(pick_back[...], third_in)
     collect(3, decoder, 1, send4, in4, halves * keep)
 
     @pl.when(decoder)
@@ -480,37 +522,73 @@
             device_id_type=MESH,
         )
 
-    def x_copy(o):
-        return pltpu.make_async_remote_copy(
-            src_ref=x_send.at[o],
-            dst_ref=x_recv.at[o],
-            send_sem=c_send.at[1],
-            recv_sem=c_x.at[o],
-            device_id=(section, dp, (xx + o) % nx * 2 + core),
-            device_id_type=MESH,
-        )
-
     def to_sibling(o):
         sib_send[o] = term((xx + o) % nx * 2 + 1 - core).astype(BF16)
         sib_copy(o).start()
 
-    turns = [o for o in (2, 1, 3, 0) if o < nx]
-    to_sibling(turns[0])
-    for k, o in enumerate(turns):
-        if k + 1 < len(turns):
-            to_sibling(turns[k + 1])
-        own = term((xx + o) % nx * 2 + core)
+    def combined(o):
+        own_term = term((xx + o) % nx * 2 + core)
         sib_copy(o).wait_recv()
-        both = own + sib_recv[o].astype(F32)
-        if o:
-            x_send[o] = both.astype(BF16)
-            x_copy(o).start()
-        else:
-            result = both
-    for o in (1, 3, 2):
-        if o < nx:
-            x_copy(o).wait_recv()
-            result = result + x_recv[o].astype(F32)
+        return own_term + sib_recv[o].astype(F32)
+
+    def part_copy(slot, o, low, size, sign):
+        return pltpu.make_async_remote_copy(
+            src_ref=x_send.at[o, pl.ds(low, size), :],
+            dst_ref=x_recv.at[o, pl.ds(low, size), :],
+            send_sem=c_send.at[1],
+            recv_sem=c_x.at[slot],
+            device_id=(section, dp, (xx + sign + nx) % nx * 2 + core),
+            device_id_type=MESH,
+        )
+
+    middle = rows // 2
+    parts_sent = []
+    if nx == 4:
+        far_up = part_copy(0, 2, 0, middle, 1)
+        far_down = part_copy(1, 2, middle, middle, -1)
+        up_plain = part_copy(2, 1, middle, middle, 1)
+        up_added = part_copy(3, 1, 0, middle, 1)
+        down_plain = part_copy(4, 3, 0, middle, -1)
+        down_added = part_copy(5, 3, middle, middle, -1)
+        parts_sent = [far_up, far_down, up_plain, up_added, down_plain, down_added]
+        to_sibling(2)
+        to_sibling(1)
+        x_send[2] = combined(2).astype(BF16)
+        far_up.start()
+        far_down.start()
+        to_sibling(3)
+        up = combined(1)
+        x_send[1, middle:, :] = up[middle:].astype(BF16)
+        up_plain.start()
+        to_sibling(0)
+        down = combined(3)
+        x_send[3, :middle, :] = down[:middle].astype(BF16)
+        down_plain.start()
+        far_up.wait_recv()
+        x_send[1, :middle, :] = (up[:middle] + x_recv[2, :middle, :].astype(F32)).astype(BF16)
+        up_added.start()
+        far_down.wait_recv()
+        x_send[3, middle:, :] = (down[middle:] + x_recv[2, middle:, :].astype(F32)).astype(BF16)
+        down_added.start()
+        result = combined(0)
+        for copy in (up_plain, down_plain, up_added, down_added):
+            copy.wait_recv()
+        result = result + x_recv[1].astype(F32) + x_recv[3].astype(F32)
+    else:
+        turns = [o for o in (1, 0) if o < nx]
+        to_sibling(turns[0])
+        for k, o in enumerate(turns):
+            if k + 1 < len(turns):
+                to_sibling(turns[k + 1])
+            result = combined(o)
+            if o:
+                x_send[o] = result.astype(BF16)
+                whole = part_copy(0, 1, 0, rows, 1)
+                whole.start()
+                parts_sent += [whole]
+        for copy in parts_sent:
+            copy.wait_recv()
+            result = result + x_recv[1].astype(F32)
     out_ref[...] = result.astype(out_ref.dtype)
 
     for kind in order:
@@ -547,18 +625,16 @@
 
     for o in range(nx):
         sib_copy(o).wait_send()
-        if o:
-            x_copy(o).wait_send()
+    for copy in parts_sent:
+        copy.wait_send()
 
 
 def shards(n_dp, n_mp, layer_rows, cotangent, norm_gains, projections, enc_len, dec_len, enc_dev, dec_dev):
     x = layer_rows[0]
     rows, features = x.shape
     depth, _, width = projections.shape[1:]
-    w = projections[0].reshape(depth, 2 * width)
     count = enc_len.shape[0]
-    tab_r = jnp.stack([enc_len, dec_len, enc_dev, dec_dev]).astype(F32)
-    tab_c = tab_r.T
+    tables = [t.reshape(1, count) for t in (enc_len, dec_len, enc_dev, dec_dev)]
     slots = 2 * n_dp
     keep = rows // slots
     quarters = 2 * width // LANES
@@ -567,13 +643,18 @@
     nz = n_dp // 2
     columns = features // n_mp
     vmem = pl.BlockSpec(memory_space=pltpu.VMEM)
+    hbm = pl.BlockSpec(memory_space=pl.ANY)
     dma = pltpu.SemaphoreType.DMA
     out = pl.pallas_call(
         functools.partial(kernel, n_dp, n_mp),
         out_shape=jax.ShapeDtypeStruct((rows, columns), BF16),
-        in_specs=[vmem] * 6,
+        in_specs=[hbm] * 4 + [vmem] * 4,
         out_specs=vmem,
         scratch_shapes=[
+            pltpu.VMEM((rows, features), BF16),
+            pltpu.VMEM((1, features), F32),
+            pltpu.VMEM((depth, 2, width), BF16),
+            pltpu.VMEM((rows, columns), BF16),
             pltpu.VMEM((features, 2 * width), BF16),
             pltpu.VMEM((features // LANES, rows, LANES), BF16),
             pltpu.VMEM((features // LANES, rows, LANES), BF16),
@@ -581,8 +662,8 @@
             pltpu.VMEM((rows, 2 * width), F32),
             pltpu.VMEM((rows, 2 * width), BF16),
             pltpu.VMEM((rows, 2 * width), BF16),
-            pltpu.VMEM((count, LANES), F32),
-            pltpu.VMEM((n_dp * halves * keep, LANES), F32),
+            pltpu.VMEM((quarters, count, n_dp * quarters * keep), BF16),
+            pltpu.VMEM((n_dp * halves * keep, n_dp * halves * EX_DEV), BF16),
             pltpu.VMEM((8, rows), F32),
             pltpu.VMEM((slots * quarters * keep, LANES), F32),
             pltpu.VMEM((slots, quarters * keep, LANES), BF16),
@@ -597,6 +678,8 @@
             pltpu.VMEM((nx, rows, columns), BF16),
             pltpu.VMEM((nx, rows, columns), BF16),
             pltpu.VMEM((nx, rows, columns), BF16),
+            dma((4,)),
+            pltpu.SemaphoreType.REGULAR,
             dma((2, 3, max(1, nz // 2))),
             dma((nz + 1,)),
             dma((2 * nx,)),
@@ -607,12 +690,12 @@
             dma((4,)),
             dma((2,)),
             dma((nx,)),
-            dma((nx,)),
+            dma((6,)),
         ],
         compiler_params=pltpu.CompilerParams(
-            collective_id=0, has_side_effects=True, vmem_limit_bytes=52 * 2**20
+            collective_id=0, has_side_effects=True, vmem_limit_bytes=60 * 2**20
         ),
-    )(x, norm_gains, w, cotangent, tab_r, tab_c)
+    )(x, norm_gains, projections[0], cotangent, *tables)
     return out[None]
 
 

time: 137 us -> 126 us (0.920)
  the two profiles are of different devices: /device:TPU:25 before, /device:TPU:17 now
where the time goes in v2:
time: 126 us
  Pallas kernels  124 us (98%)
  local copies, waits for them, and re-layouts  1.67 us (1%)
    pallas_call x1, Pallas kernels, shards(): pl.pallas_call(functools.partial(kernel, n_dp, n_mp), out_shape=jax.Shape...  124 us

profile of v2, /device:TPU:17, one launch (start us, length us, event | category | flops | bytes accessed | tf_op | source)
XLA Modules:
  0.0 125.8 jit_solution(233963708235946213)
XLA Ops:
  0.0 124.2 %shard_map.82 = bf16[256,512]{1,0:T(8,128)(2,1)} custom-call(bf16[256,4096]{1,0:T(8,128)(2,1)} %bitcast.7, f32[1,4096]{1,0:T(1,128)} %gain_hbm.1, bf16[128,2,256]{2,1,0:T(2,128)(2,1)} %bitcast.9, bf16[256,512]{1,0:T(8,128)(2,1)} %cot_hbm.1, s32[1,256]{1,0:T(1,128)} %bitcast.10, s32[1,256]{1,0:T(1,128)} %bitcast.11, s32[1,256]{1,0:T(1,128)} %bitcast.12, ...), custom_call_target="tpu_custom_call" | custom-call | tf_op jit(solution)/shard_map/pallas_call | solution.py:648
  124.2 1.7 %copy.10 = bf16[1,256,512]{2,1,0:T(8,128)(2,1)} copy(bf16[1,256,512]{2,1,0:T(8,128)(2,1)} %bitcast.8) | data formatting | bytes 524288

commit v3 on v2

--- a/solution.py
+++ b/solution.py
@@ -11,7 +11,7 @@
 EX_DEV = 8
 EPS = 1e-06
 LANES = 128
-CUT = 48
+CUT = 64
 MESH = pl.DeviceIdType.MESH
 F32 = jnp.float32
 BF16 = jnp.bfloat16
@@ -53,17 +53,14 @@
     qkv,
     grad,
     pick_ref,
-    pick_back,
-    rank_ref,
+    own_ref,
+    far_ref,
+    probs_ref,
     wide,
     send1,
     in1,
     send2,
     in2,
-    send3,
-    in3,
-    send4,
-    in4,
     sib_send,
     sib_recv,
     x_send,
@@ -85,12 +82,11 @@
     nz = n_dp // 2
     nx = n_mp // 2
     half = nz // 2
-    slots = 2 * n_dp
     rows, features = x_ref.shape
     depth, _, width = w_ref.shape
-    keep = rows // slots
-    quarters = 2 * width // LANES
-    halves = width // LANES
+    keep = rows // n_dp
+    turns = 2 * rows // EX_DEV // n_dp
+    sides = width // LANES
     section = lax.axis_index("section")
     dp = lax.axis_index("dp")
     mp = lax.axis_index("mp")
@@ -98,7 +94,6 @@
     z = dp % nz
     xx = mp // 2
     core = mp % 2
-    me = section * n_dp + dp
     encoder = section == 0
     decoder = section == 1
 
@@ -220,71 +215,97 @@
                 left1[c, at, :] = normed[:, c * LANES : (c + 1) * LANES]
 
     count = EX_DEV * n_dp
-    el_r, dl_r, ed_r, dd_r = (t[...].astype(F32) for t in (el_ref, dl_ref, ed_ref, dd_ref))
+    far_rows = n_dp * turns * EX_DEV
+    enc_r = tuple(t[...].astype(F32) for t in (el_ref, ed_ref))
+    dec_r = tuple(t[...].astype(F32) for t in (dl_ref, dd_ref))
+    len_r, dev_r = (jnp.where(encoder, a, b) for a, b in zip(enc_r, dec_r))
+    far_len_r, far_dev_r = (jnp.where(encoder, b, a) for a, b in zip(enc_r, dec_r))
+    here = dp.astype(F32)
     found = {}
 
     def starts():
         shape = (count, count)
         down = lax.broadcasted_iota(jnp.int32, shape, 0).astype(F32)
         along = lax.broadcasted_iota(jnp.int32, shape, 1).astype(F32)
+        one = jnp.ones(shape, F32)
 
         def column(row):
             return jnp.sum(jnp.where(down == along, row, 0.0), axis=1, keepdims=True)
 
-        el_c, dl_c, ed_c, dd_c = (column(t) for t in (el_r, dl_r, ed_r, dd_r))
-        same_enc = ed_r == ed_c
-        same_dec = dd_r == dd_c
-        one = jnp.ones(shape, F32)
-        dstart_r = jnp.sum(
-            jnp.where(same_dec & (down < along), dl_c * one, 0.0), axis=0, keepdims=True
-        )
-        rank_r = jnp.sum(jnp.where(same_enc & (down < along), one, 0.0), axis=0, keepdims=True)
-        estart_c = jnp.sum(
-            jnp.where(same_enc & (along < down), el_r * one, 0.0), axis=1, keepdims=True
-        )
-        rank_c = jnp.sum(jnp.where(same_enc & (along < down), one, 0.0), axis=1, keepdims=True)
-        found.update(down=down, dstart_r=dstart_r, rank_r=rank_r)
+        len_c, dev_c, far_len_c, far_dev_c = (
+            column(t) for t in (len_r, dev_r, far_len_r, far_dev_r)
+        )
+        above = (dev_r == dev_c) & (down < along)
+        before = (dev_r == dev_c) & (along < down)
+        found.update(
+            down=down,
+            len_c=len_c,
+            dev_c=dev_c,
+            far_len_c=far_len_c,
+            start_r=jnp.sum(jnp.where(above, len_c * one, 0.0), axis=0, keepdims=True),
+            rank_r=jnp.sum(jnp.where(above, one, 0.0), axis=0, keepdims=True),
+            start_c=jnp.sum(jnp.where(before, len_r * one, 0.0), axis=1, keepdims=True),
+            rank_c=jnp.sum(jnp.where(before, one, 0.0), axis=1, keepdims=True),
+            far_rank_r=jnp.sum(
+                jnp.where((far_dev_r == far_dev_c) & (down < along), one, 0.0),
+                axis=0,
+                keepdims=True,
+            ),
+            far_start_c=jnp.sum(
+                jnp.where((far_dev_r == far_dev_c) & (along < down), far_len_r * one, 0.0),
+                axis=1,
+                keepdims=True,
+            ),
+        )
+
+    def own_ranks():
         u_r = lax.broadcasted_iota(jnp.int32, (count, rows), 1).astype(F32)
-        mine = (ed_c == dp.astype(F32)) & (estart_c <= u_r) & (u_r < estart_c + el_c)
-        rank_u = jnp.sum(jnp.where(mine, rank_c * jnp.ones_like(u_r), 0.0), axis=0, keepdims=True)
-        rank_ref[...] = jnp.broadcast_to(rank_u, rank_ref.shape)
-
-    def pick_rows():
-        start_i = found["dstart_r"].astype(jnp.int32)
-        offset = (me - start_i) & (slots - 1)
-        slot = (start_i + offset) // slots
-        source = dd_r * float(quarters * keep) + slot.astype(F32)
-        value = jnp.where(offset.astype(F32) < dl_r, source + 1.0, 0.0)
-        place = ed_r * float(EX_DEV) + found["rank_r"]
+        start_c, start_r = found["start_c"], found["start_r"]
+        mine = (found["dev_c"] == here) & (start_c <= u_r) & (u_r < start_c + found["len_c"])
+        along = jnp.sum(
+            jnp.where(mine, found["rank_c"] * jnp.ones_like(u_r), 0.0), axis=0, keepdims=True
+        )
+        u_c = lax.broadcasted_iota(jnp.int32, (rows, count), 0).astype(F32)
+        mine = (dev_r == here) & (start_r <= u_c) & (u_c < start_r + len_r)
+        down = jnp.sum(
+            jnp.where(mine, found["rank_r"] * jnp.ones_like(u_c), 0.0), axis=1, keepdims=True
+        )
+        far_ref[:, :rows] = jnp.broadcast_to(along, (far_ref.shape[0], rows))
+        own_ref[...] = jnp.broadcast_to(down, own_ref.shape)
+
+    def far_ranks():
+        c_i = lax.broadcasted_iota(jnp.int32, (count, far_rows), 1)
+        rank = (c_i % EX_DEV).astype(F32)
+        hit = (found["dev_c"] == here) & (found["rank_c"] == rank)
+        one = jnp.ones_like(rank)
+        start = jnp.sum(jnp.where(hit, found["far_start_c"] * one, 0.0), axis=0, keepdims=True)
+        length = jnp.sum(jnp.where(hit, found["far_len_c"] * one, 0.0), axis=0, keepdims=True)
+        c_r = lax.broadcasted_iota(jnp.int32, (1, far_rows), 1)
+        offset = (c_r // (turns * EX_DEV) - start.astype(jnp.int32)) & (n_dp - 1)
+        offset = offset + c_r % (turns * EX_DEV) // EX_DEV * n_dp
+        rank_r = jnp.where(offset.astype(F32) < length, (c_r % EX_DEV).astype(F32), -1.0)
+
+        @pl.when(decoder)
+        def _():
+            far_ref[...] = jnp.broadcast_to(rank_r, far_ref.shape)
+
+    def pick_rows(turn):
+        start_i = found["start_r"].astype(jnp.int32)
+        offset = ((dp - start_i) & (n_dp - 1)) + turn * n_dp
+        source = dev_r * float(sides * keep) + ((start_i + offset) // n_dp).astype(F32)
+        value = jnp.where(offset.astype(F32) < len_r, source + 1.0, 0.0)
+        place = far_dev_r * float(EX_DEV) + found["far_rank_r"]
         down = found["down"]
-        found["fidx"] = (
-            jnp.sum(jnp.where(place == down, value * jnp.ones_like(down), 0.0), axis=1, keepdims=True)
-            - 1.0
-        )
-
-    def pick_side(b):
-        fidx = found["fidx"]
-        place = lax.broadcasted_iota(
-            jnp.int32, (n_dp * EX_DEV, n_dp * quarters * keep), 1
-        ).astype(F32)
+        one = jnp.ones_like(down)
+        found[turn] = (
+            jnp.sum(jnp.where(place == down, value * one, 0.0), axis=1, keepdims=True) - 1.0
+        )
+
+    def pick_side(b, turn):
+        fidx = found[turn]
+        place = lax.broadcasted_iota(jnp.int32, (count, n_dp * sides * keep), 1).astype(F32)
         at = jnp.where(fidx >= 0.0, fidx + float(b * keep), -1.0)
-        pick_ref[b] = jnp.where(place == at, 1.0, 0.0).astype(BF16)
-
-    def pick_back_rows():
-        q_i = lax.broadcasted_iota(jnp.int32, (n_dp * halves * keep, count), 0)
-        dev_q = (q_i // (halves * keep)).astype(F32)
-        side_q = (q_i % (halves * keep) // keep).astype(F32)
-        row_q = (q_i % keep * slots + me).astype(F32)
-        dstart_r = found["dstart_r"]
-        hit = (dd_r == dev_q) & (dstart_r <= row_q) & (row_q < dstart_r + dl_r)
-        target = (
-            ed_r * float(halves * EX_DEV) + found["rank_r"] + side_q * float(EX_DEV) + 1.0
-        )
-        ridx = jnp.sum(jnp.where(hit, target, 0.0), axis=1, keepdims=True) - 1.0
-        place = lax.broadcasted_iota(
-            jnp.int32, (n_dp * halves * keep, n_dp * halves * EX_DEV), 1
-        ).astype(F32)
-        pick_back[...] = jnp.where(place == ridx, 1.0, 0.0).astype(BF16)
+        pick_ref[b * turns + turn] = jnp.where(place == at, 1.0, 0.0).astype(BF16)
 
     def product(y, zb):
         total0 = total1 = None
@@ -323,8 +344,8 @@
 
     acc[...] = jnp.zeros_like(acc)
     items = [first_norm] + [functools.partial(norm_rows, i) for i in range(1, rows // step)]
-    items += [starts, pick_rows] + [functools.partial(pick_side, b) for b in range(quarters)]
-    items += [pick_back_rows]
+    items += [starts, own_ranks, far_ranks] + [functools.partial(pick_rows, t) for t in range(turns)]
+    items += [functools.partial(pick_side, b, t) for b in range(sides) for t in range(turns)]
     late = [functools.partial(cot_pass, o) for o in (1, 3, 2) if o < nx] + [cot_wait]
     late += [functools.partial(arrived, 1, 0)]
     for hop in range(1, half + 1):
@@ -347,159 +368,135 @@
         item()
 
     pl.semaphore_signal(cross_sem, inc=1, device_id=(across, dp, mp), device_id_type=MESH)
-    pl.semaphore_wait(cross_sem, 1)
-
-    def hop_send_copy(k, src, dst, target_section, target_dp):
+
+    def hop_copy(k, src, dst, target_section, target):
         return pltpu.make_async_remote_copy(
             src_ref=src,
             dst_ref=dst,
             send_sem=hop_send.at[k],
             recv_sem=hop_recv.at[k],
-            device_id=(target_section, target_dp, mp),
+            device_id=(target_section, target, mp),
             device_id_type=MESH,
         )
 
-    def block_of(buf, i, size):
-        if size is None:
-            return buf.at[i]
-        return buf.at[pl.ds(pl.multiple_of(i * size, size), size)]
-
-    def wait_bytes(sem, buf, count, size):
-        part = buf.at[pl.ds(0, count if size is None else count * size)]
-        pltpu.make_async_copy(part, part, sem).wait()
-
-    def spread(k, is_source, src, dst, size=None):
-        @pl.when(is_source)
-        def _():
-            pltpu.make_async_copy(
-                block_of(src, me, size), block_of(dst, dp, size), hop_local.at[k]
-            ).start()
-
-            run = 9 if (slots - 1) % 9 == 0 else 1
-
-            def some(g, carry):
-                for r in range(run):
-                    i = (me + 1 + g * run + r) & (slots - 1)
-                    hop_send_copy(
-                        k,
-                        block_of(src, i, size),
-                        block_of(dst, dp, size),
-                        i // n_dp,
-                        i & (n_dp - 1),
-                    ).start()
-                return carry
-
-            lax.fori_loop(0, (slots - 1) // run, some, 0)
-            pltpu.make_async_copy(
-                block_of(src, me, size), block_of(dst, dp, size), hop_local.at[k]
-            ).wait()
-            wait_bytes(hop_recv.at[k], dst, n_dp - 1, size)
-
-        @pl.when(jnp.logical_not(is_source))
-        def _():
-            wait_bytes(hop_recv.at[k], dst, n_dp, size)
-
-    def collect(k, is_target, target_section, src, dst, size=None):
-        def one(j):
-            t = (dp + j) & (n_dp - 1)
-            hop_send_copy(
-                k, block_of(src, t, size), block_of(dst, me, size), target_section, t
-            ).start()
-
-        run = 10 if (n_dp - 2) % 10 == 0 else 1
-
-        def some(g, carry):
-            for r in range(run):
-                one(1 + g * run + r)
-            return carry
-
-        @pl.when(is_target)
-        def _():
-            pltpu.make_async_copy(
-                block_of(src, dp, size), block_of(dst, me, size), hop_local.at[k]
-            ).start()
-
-        lax.fori_loop(0, (n_dp - 2) // run, some, 0)
-        one(n_dp - 1)
-
-        @pl.when(jnp.logical_not(is_target))
-        def _():
-            one(0)
-
-        @pl.when(is_target)
-        def _():
-            pltpu.make_async_copy(
-                block_of(src, dp, size), block_of(dst, me, size), hop_local.at[k]
-            ).wait()
-            wait_bytes(hop_recv.at[k], dst, slots - 1, size)
+    def wait_bytes(sem, buf, size):
+        pltpu.make_async_copy(buf.at[pl.ds(0, size)], buf.at[pl.ds(0, size)], sem).wait()
+
+    def local_copy(part):
+        return pltpu.make_async_copy(
+            send1.at[part, dp], in1.at[part, dp], hop_local.at[part]
+        )
 
     qkv[...] = acc[...].astype(BF16)
+    for part in range(2):
+        for b in range(sides):
+            low = part * width + b * LANES
+            for a in range(keep):
+                wide[pl.ds(b * keep + a, n_dp, stride=sides * keep), :] = qkv[
+                    a * n_dp : (a + 1) * n_dp, low : low + LANES
+                ].astype(F32)
+        send1[part] = wide[...].astype(BF16).reshape(n_dp, sides * keep, LANES)
+        local_copy(part).start()
+        for j in range(1, n_dp):
+            target = (dp + j) & (n_dp - 1)
+            hop_copy(part, send1.at[part, target], in1.at[part, dp], section, target).start()
+
+    for part in range(2):
+        local_copy(part).wait()
+        wait_bytes(hop_recv.at[part], in1.at[part], n_dp - 1)
+        first_in = in1[part].reshape(n_dp * sides * keep, LANES)
+        pieces = [
+            nn(pick_ref[k], first_in).reshape(n_dp, EX_DEV, LANES) for k in range(sides * turns)
+        ]
+        send2[part] = jnp.concatenate(pieces, axis=1).astype(BF16)
+        if part == 0:
+            pl.semaphore_wait(cross_sem, 1)
+        for j in range(n_dp):
+            target = (dp + j) & (n_dp - 1)
+            hop_copy(2 + part, send2.at[part, target], in2.at[part, dp], across, target).start()
+
+    scale = 1.0 / float(HEAD) ** 0.5
+    lane = lax.broadcasted_iota(jnp.int32, (1, LANES), 1) // HEAD
+    heads = LANES // HEAD
+    per_side = turns * EX_DEV
+
+    def came(part, b):
+        return in2[part, :, b * per_side : (b + 1) * per_side, :].reshape(far_rows, LANES)
+
+    def own(part, b):
+        return qkv[:, part * width + b * LANES : part * width + (b + 1) * LANES]
+
+    def one_head(t, s):
+        return jnp.where(lane == s, t, jnp.zeros_like(t))
+
+    def softmax(q, k, mask):
+        weight = jnp.where(mask, jnp.exp(nt(q, k) * scale), 0.0)
+        return weight * (1.0 / jnp.sum(weight, axis=1, keepdims=True))
+
+    def backward(probs, dout_s, v):
+        probs_bf = probs.astype(BF16)
+        attended = nn(probs_bf, v).astype(BF16)
+        delta = jnp.sum(dout_s.astype(F32) * attended.astype(F32), axis=1, keepdims=True)
+        return probs_bf, (probs * (nt(dout_s, v) - delta) * scale).astype(BF16)
+
+    def merge(news, sums, s):
+        return [jnp.where(lane == s, new, old) for new, old in zip(news, sums)] if s else news
+
+    wait_bytes(hop_recv.at[2], in2.at[0], n_dp)
+
+    @pl.when(encoder)
+    def _():
+        example = lax.broadcasted_iota(jnp.int32, (far_rows, rows), 0) % EX_DEV
+        mask = example.astype(F32) == far_ref[:1, :rows]
+        for b in range(sides):
+            q = came(0, b)
+            for s in range(heads):
+                probs_ref[b * heads + s] = softmax(one_head(q, s), own(0, b), mask)
 
     @pl.when(decoder)
     def _():
-        for b in range(quarters):
-            for a in range(keep):
-                wide[pl.ds(b * keep + a, slots, stride=quarters * keep), :] = qkv[
-                    a * slots : (a + 1) * slots, b * LANES : (b + 1) * LANES
-                ].astype(F32)
-        send1[...] = wide[...].astype(BF16).reshape(send1.shape)
-
-    spread(0, decoder, send1, in1)
-
-    first_in = in1[...].reshape(n_dp * quarters * keep, LANES)
-    pieces = [nn(pick_ref[b], first_in).reshape(n_dp, EX_DEV, LANES) for b in range(quarters)]
-    send2[...] = jnp.concatenate(pieces, axis=1).astype(BF16)
-    collect(1, encoder, 0, send2, in2)
+        mask = own_ref[:, :1] == far_ref[:1, :]
+        for b in range(sides):
+            k = came(0, b)
+            for s in range(heads):
+                probs = softmax(one_head(own(0, b), s), k, mask)
+                for c in range(far_rows // rows):
+                    probs_ref[b * heads + s, c * rows : (c + 1) * rows, :] = probs[
+                        :, c * rows : (c + 1) * rows
+                    ]
+
+    wait_bytes(hop_recv.at[3], in2.at[1], n_dp)
 
     @pl.when(encoder)
     def _():
-        scale = 1.0 / float(HEAD) ** 0.5
-        total = slots * EX_DEV
-        incoming = in2[...].astype(F32)
-        parts = [
-            incoming[:, b * EX_DEV : (b + 1) * EX_DEV, :].reshape(total, LANES).astype(BF16)
-            for b in range(quarters)
-        ]
-        example = (lax.broadcasted_iota(jnp.int32, (total, rows), 0) % EX_DEV).astype(F32)
-        mask = example == rank_ref[:1, :]
-        back = []
-        lane = lax.broadcasted_iota(jnp.int32, (1, LANES), 1) // HEAD
-        for b in range(halves):
-            q, dout = parts[b], parts[halves + b]
-            k = qkv[:, b * LANES : (b + 1) * LANES]
-            v = qkv[:, width + b * LANES : width + (b + 1) * LANES]
+        for b in range(sides):
+            q, dout = came(0, b), came(1, b)
             sums = []
-            for s in range(LANES // HEAD):
-                here = lane == s
-                q_s = jnp.where(here, q, jnp.zeros_like(q))
-                dout_s = jnp.where(here, dout, jnp.zeros_like(dout))
-                weight = jnp.where(mask, jnp.exp(nt(q_s, k) * scale), 0.0)
-                probs = weight * (1.0 / jnp.sum(weight, axis=1, keepdims=True))
-                probs_bf = probs.astype(BF16)
-                attended = nn(probs_bf, v).astype(BF16)
-                delta = jnp.sum(
-                    dout_s.astype(F32) * attended.astype(F32), axis=1, keepdims=True
+            for s in range(heads):
+                probs_bf, dscore = backward(
+                    probs_ref[b * heads + s], one_head(dout, s), own(1, b)
                 )
-                dscore = (probs * (nt(dout_s, v) - delta) * scale).astype(BF16)
-                news = (nn(dscore, k), tn(dscore, q), tn(probs_bf, dout))
-                sums = [jnp.where(here, new, old) for new, old in zip(news, sums)] if s else news
-            grad[:, b * LANES : (b + 1) * LANES] = sums[1].astype(BF16)
-            grad[:, width + b * LANES : width + (b + 1) * LANES] = sums[2].astype(BF16)
-            back += [sums[0].reshape(slots, EX_DEV, LANES)]
-        send3[...] = jnp.concatenate(back, axis=1).astype(BF16)
-
-    spread(2, encoder, send3, in3)
-    third_in = in3[...].reshape(n_dp * halves * EX_DEV, LANES)
-    send4[...] = nn(pick_back[...], third_in)
-    collect(3, decoder, 1, send4, in4, halves * keep)
+                sums = merge((tn(dscore, q), tn(probs_bf, dout)), sums, s)
+            for part in range(2):
+                low = part * width + b * LANES
+                grad[:, low : low + LANES] = sums[part].astype(BF16)
 
     @pl.when(decoder)
     def _():
-        for b in range(halves):
-            for a in range(keep):
-                grad[a * slots : (a + 1) * slots, b * LANES : (b + 1) * LANES] = in4[
-                    pl.ds(b * keep + a, slots, stride=halves * keep), :
-                ].astype(BF16)
+        for b in range(sides):
+            k, v = came(0, b), came(1, b)
+            sums = []
+            for s in range(heads):
+                probs = jnp.concatenate(
+                    [
+                        probs_ref[b * heads + s, c * rows : (c + 1) * rows, :]
+                        for c in range(far_rows // rows)
+                    ],
+                    axis=1,
+                )
+                dscore = backward(probs, one_head(own(1, b), s), v)[1]
+                sums = merge((nn(dscore, k),), sums, s)
+            grad[:, b * LANES : (b + 1) * LANES] = sums[0].astype(BF16)
         grad[:, width:] = jnp.zeros((rows, width), BF16)
 
     columns = features // n_mp
@@ -608,21 +605,9 @@
         for o in range(1, 2 * nx):
             cot_copy(mp, o, sibling).wait_send()
 
-    def sent(k, buf, count, size=None):
-        wait_bytes(hop_send.at[k], buf, count, size)
-
-    @pl.when(decoder)
-    def _():
-        sent(0, send1, slots - 1)
-        sent(1, send2, n_dp)
-        sent(3, send4, n_dp - 1, halves * keep)
-
-    @pl.when(encoder)
-    def _():
-        sent(1, send2, n_dp - 1)
-        sent(2, send3, slots - 1)
-        sent(3, send4, n_dp, halves * keep)
-
+    for part in range(2):
+        wait_bytes(hop_send.at[part], send1.at[part], n_dp - 1)
+        wait_bytes(hop_send.at[2 + part], send2.at[part], n_dp)
     for o in range(nx):
         sib_copy(o).wait_send()
     for copy in parts_sent:
@@ -635,10 +620,10 @@
     depth, _, width = projections.shape[1:]
     count = enc_len.shape[0]
     tables = [t.reshape(1, count) for t in (enc_len, dec_len, enc_dev, dec_dev)]
-    slots = 2 * n_dp
-    keep = rows // slots
-    quarters = 2 * width // LANES
-    halves = width // LANES
+    keep = rows // n_dp
+    turns = 2 * rows // EX_DEV // n_dp
+    sides = width // LANES
+    far_rows = n_dp * turns * EX_DEV
     nx = n_mp // 2
     nz = n_dp // 2
     columns = features // n_mp
@@ -662,18 +647,15 @@
             pltpu.VMEM((rows, 2 * width), F32),
             pltpu.VMEM((rows, 2 * width), BF16),
             pltpu.VMEM((rows, 2 * width), BF16),
-            pltpu.VMEM((quarters, count, n_dp * quarters * keep), BF16),
-            pltpu.VMEM((n_dp * halves * keep, n_dp * halves * EX_DEV), BF16),
-            pltpu.VMEM((8, rows), F32),
-            pltpu.VMEM((slots * quarters * keep, LANES), F32),
-            pltpu.VMEM((slots, quarters * keep, LANES), BF16),
-            pltpu.VMEM((n_dp, quarters * keep, LANES), BF16),
-            pltpu.VMEM((n_dp, quarters * EX_DEV, LANES), BF16),
-            pltpu.VMEM((slots, quarters * EX_DEV, LANES), BF16),
-            pltpu.VMEM((slots, halves * EX_DEV, LANES), BF16),
-            pltpu.VMEM((n_dp, halves * EX_DEV, LANES), BF16),
-            pltpu.VMEM((n_dp * halves * keep, LANES), F32),
-            pltpu.VMEM((slots * halves * keep, LANES), F32),
+            pltpu.VMEM((sides * turns, count, n_dp * sides * keep), BF16),
+            pltpu.VMEM((rows, LANES), F32),
+            pltpu.VMEM((8, far_rows), F32),
+            pltpu.VMEM((sides * LANES // HEAD, far_rows, rows), F32),
+            pltpu.VMEM((n_dp * sides * keep, LANES), F32),
+            pltpu.VMEM((2, n_dp, sides * keep, LANES), BF16),
+            pltpu.VMEM((2, n_dp, sides * keep, LANES), BF16),
+            pltpu.VMEM((2, n_dp, sides * turns * EX_DEV, LANES), BF16),
+            pltpu.VMEM((2, n_dp, sides * turns * EX_DEV, LANES), BF16),
             pltpu.VMEM((nx, rows, columns), BF16),
             pltpu.VMEM((nx, rows, columns), BF16),
             pltpu.VMEM((nx, rows, columns), BF16),
@@ -687,7 +669,7 @@
             dma,
             dma((4,)),
             dma((4,)),
-            dma((4,)),
+            dma((2,)),
             dma((2,)),
             dma((nx,)),
             dma((6,)),

time: 126 us -> 111 us (0.88)
  the two profiles are of different devices: /device:TPU:17 before, /device:TPU:1 now
where the time goes in v3:
time: 111 us; the launch traced here: 110 us
  Pallas kernels  109 us (98%)
  local copies, waits for them, and re-layouts  1.67 us (2%)
    pallas_call x1, Pallas kernels, shards(): pl.pallas_call(functools.partial(kernel, n_dp, n_mp), out_shape=jax.Shape...  109 us

profile of v3, /device:TPU:1, one launch (start us, length us, event | category | flops | bytes accessed | tf_op | source)
XLA Modules:
  0.0 110.4 jit_solution(13858312617026112884)
XLA Ops:
  0.0 108.7 %shard_map.82 = bf16[256,512]{1,0:T(8,128)(2,1)} custom-call(bf16[256,4096]{1,0:T(8,128)(2,1)} %bitcast.7, f32[1,4096]{1,0:T(1,128)} %gain_hbm.1, bf16[128,2,256]{2,1,0:T(2,128)(2,1)} %bitcast.9, bf16[256,512]{1,0:T(8,128)(2,1)} %cot_hbm.1, s32[1,256]{1,0:T(1,128)} %bitcast.10, s32[1,256]{1,0:T(1,128)} %bitcast.11, s32[1,256]{1,0:T(1,128)} %bitcast.12, ...), custom_call_target="tpu_custom_call" | custom-call | tf_op jit(solution)/shard_map/pallas_call | solution.py:633
  108.7 1.7 %copy.10 = bf16[1,256,512]{2,1,0:T(8,128)(2,1)} copy(bf16[1,256,512]{2,1,0:T(8,128)(2,1)} %bitcast.8) | data formatting | bytes 524288

commit v4 on v3

--- a/solution.py
+++ b/solution.py
@@ -56,7 +56,7 @@
     own_ref,
     far_ref,
     probs_ref,
-    wide,
+    spread_ref,
     send1,
     in1,
     send2,
@@ -110,7 +110,7 @@
     across = 1 - section
     greeted = [(section, yl * nz + (z + 1) % nz, mp), (section, yl * nz + (z + nz - 1) % nz, mp)]
     greeted += [(section, (1 - yl) * nz + z, mp), (across, dp, mp), (section, dp, sibling)]
-    greeted += [(section, dp, (xx + o) % nx * 2 + core) for o in range(1, nx)]
+    greeted += [(section, dp, ((xx + o) & (nx - 1)) * 2 + core) for o in range(1, nx)]
     barrier = pltpu.get_barrier_semaphore()
     for target in greeted:
         pl.semaphore_signal(barrier, inc=1, device_id=target, device_id_type=MESH)
@@ -135,13 +135,13 @@
     def z_copy(sign, kind, hop, sending):
         y = 1 - yl if kind == "o" else yl
         back = hop - 1 if sending else hop
-        part = span(kind, y, (z - sign * back + nz) % nz)
+        part = span(kind, y, (z - sign * back) & (nz - 1))
         return pltpu.make_async_remote_copy(
             src_ref=part,
             dst_ref=part,
             send_sem=w_send_sem,
             recv_sem=z_sems.at[(1 - sign) // 2, order.index(kind), hop - 1],
-            device_id=(section, yl * nz + (z + sign + nz) % nz, mp),
+            device_id=(section, yl * nz + ((z + sign) & (nz - 1)), mp),
             device_id_type=MESH,
         )
 
@@ -152,7 +152,7 @@
 
     def y_copy(kind, sign, hop, sending):
         y = yl if sending else 1 - yl
-        part = span(kind, y, (z - sign * hop + nz) % nz)
+        part = span(kind, y, (z - sign * hop) & (nz - 1))
         slot = nz if kind == "a" else y_slot(sign, hop)
         return pltpu.make_async_remote_copy(
             src_ref=part,
@@ -190,7 +190,7 @@
             left1[mp * per_mp + c] = cot_ref[:, c * LANES : (c + 1) * LANES]
         for o in (2, 1, 3):
             if o < nx:
-                cot_copy(mp, o, (xx + o) % nx * 2 + core).start()
+                cot_copy(mp, o, ((xx + o) & (nx - 1)) * 2 + core).start()
         cot_copy(mp, nx, sibling).start()
 
     y_copy("a", 1, 0, False).wait_recv()
@@ -289,6 +289,12 @@
         def _():
             far_ref[...] = jnp.broadcast_to(rank_r, far_ref.shape)
 
+    def spread_rows():
+        sent = lax.broadcasted_iota(jnp.int32, (rows, rows), 0)
+        row = lax.broadcasted_iota(jnp.int32, (rows, rows), 1)
+        here_too = sent % keep * n_dp + sent // keep == row
+        spread_ref[...] = jnp.where(here_too, 1.0, 0.0).astype(BF16)
+
     def pick_rows(turn):
         start_i = found["start_r"].astype(jnp.int32)
         offset = ((dp - start_i) & (n_dp - 1)) + turn * n_dp
@@ -321,7 +327,7 @@
 
     def arrived(sign, hop):
         y_copy("b", sign, hop, False).wait_recv()
-        product(yl, (z - sign * hop + nz) % nz)
+        product(yl, (z - sign * hop) & (nz - 1))
 
     def cot_pass(o):
         @pl.when(decoder)
@@ -344,7 +350,7 @@
 
     acc[...] = jnp.zeros_like(acc)
     items = [first_norm] + [functools.partial(norm_rows, i) for i in range(1, rows // step)]
-    items += [starts, own_ranks, far_ranks] + [functools.partial(pick_rows, t) for t in range(turns)]
+    items += [spread_rows, starts, own_ranks, far_ranks] + [functools.partial(pick_rows, t) for t in range(turns)]
     items += [functools.partial(pick_side, b, t) for b in range(sides) for t in range(turns)]
     late = [functools.partial(cot_pass, o) for o in (1, 3, 2) if o < nx] + [cot_wait]
     late += [functools.partial(arrived, 1, 0)]
@@ -382,24 +388,36 @@
     def wait_bytes(sem, buf, size):
         pltpu.make_async_copy(buf.at[pl.ds(0, size)], buf.at[pl.ds(0, size)], sem).wait()
 
+    def to_all(send):
+        def four(k, carry):
+            away = half - 1 - k
+            for sign in (1, -1):
+                for y in (yl, 1 - yl):
+                    send(y * nz + ((z + sign * away) & (nz - 1)))
+            return carry
+
+        for y in (yl, 1 - yl):
+            send(y * nz + ((z + half) & (nz - 1)))
+        lax.fori_loop(0, half - 1, four, 0)
+
     def local_copy(part):
         return pltpu.make_async_copy(
             send1.at[part, dp], in1.at[part, dp], hop_local.at[part]
         )
 
-    qkv[...] = acc[...].astype(BF16)
     for part in range(2):
-        for b in range(sides):
-            low = part * width + b * LANES
-            for a in range(keep):
-                wide[pl.ds(b * keep + a, n_dp, stride=sides * keep), :] = qkv[
-                    a * n_dp : (a + 1) * n_dp, low : low + LANES
-                ].astype(F32)
-        send1[part] = wide[...].astype(BF16).reshape(n_dp, sides * keep, LANES)
+        at = slice(part * width, (part + 1) * width)
+        qkv[:, at] = acc[:, at].astype(BF16)
+        moved = nn(spread_ref[...], qkv[:, at]).reshape(n_dp, keep, width)
+        pieces = [moved[:, :, b * LANES : (b + 1) * LANES] for b in range(sides)]
+        send1[part] = jnp.concatenate(pieces, axis=1).astype(BF16)
         local_copy(part).start()
-        for j in range(1, n_dp):
-            target = (dp + j) & (n_dp - 1)
+
+        def send_to(target, part=part):
             hop_copy(part, send1.at[part, target], in1.at[part, dp], section, target).start()
+
+        to_all(send_to)
+        send_to((1 - yl) * nz + z)
 
     for part in range(2):
         local_copy(part).wait()
@@ -411,9 +429,13 @@
         send2[part] = jnp.concatenate(pieces, axis=1).astype(BF16)
         if part == 0:
             pl.semaphore_wait(cross_sem, 1)
-        for j in range(n_dp):
-            target = (dp + j) & (n_dp - 1)
+
+        def pass_to(target, part=part):
             hop_copy(2 + part, send2.at[part, target], in2.at[part, dp], across, target).start()
+
+        to_all(pass_to)
+        pass_to(dp)
+        pass_to((1 - yl) * nz + z)
 
     scale = 1.0 / float(HEAD) ** 0.5
     lane = lax.broadcasted_iota(jnp.int32, (1, LANES), 1) // HEAD
@@ -441,6 +463,17 @@
 
     def merge(news, sums, s):
         return [jnp.where(lane == s, new, old) for new, old in zip(news, sums)] if s else news
+
+    over_z = (nz - 1) * (depth + CUT)
+    over_y = CUT + nz * (depth - CUT)
+    wait_bytes(w_send_sem, wall, over_z)
+    wait_bytes(w_send_sem, wall, over_y)
+    for part in range(2):
+        wait_bytes(hop_send.at[part], send1.at[part], n_dp - 1)
+
+    @pl.when(decoder)
+    def _():
+        wait_bytes(cot_send_sem, left1, (2 * nx - 1) * per_mp)
 
     wait_bytes(hop_recv.at[2], in2.at[0], n_dp)
 
@@ -504,29 +537,36 @@
     inverse = inv_ref[:, :1]
     slope = inverse * inverse * share * (1.0 / features)
 
-    def term(owner):
+    def term(owner, low, size):
         at = pl.ds(pl.multiple_of(owner * columns, columns), columns)
-        raw = nt(grad[...], wall[at, :])
-        return inverse * (raw * gain_ref[:, at]) - x_ref[:, at].astype(F32) * slope
-
-    def sib_copy(o):
+        here_rows = slice(low, low + size)
+        raw = nt(grad[here_rows, :], wall[at, :])
+        return inverse[here_rows] * (raw * gain_ref[:, at]) - x_ref[
+            here_rows, at
+        ].astype(F32) * slope[here_rows]
+
+    middle = rows // 2
+
+    def sib_copy(o, h):
+        at = pl.ds(h * middle, middle)
         return pltpu.make_async_remote_copy(
-            src_ref=sib_send.at[o],
-            dst_ref=sib_recv.at[o],
+            src_ref=sib_send.at[o, at, :],
+            dst_ref=sib_recv.at[o, at, :],
             send_sem=c_send.at[0],
-            recv_sem=c_sib.at[o],
+            recv_sem=c_sib.at[o, h],
             device_id=(section, dp, sibling),
             device_id_type=MESH,
         )
 
-    def to_sibling(o):
-        sib_send[o] = term((xx + o) % nx * 2 + 1 - core).astype(BF16)
-        sib_copy(o).start()
-
-    def combined(o):
-        own_term = term((xx + o) % nx * 2 + core)
-        sib_copy(o).wait_recv()
-        return own_term + sib_recv[o].astype(F32)
+    def to_sibling(o, h):
+        at = slice(h * middle, (h + 1) * middle)
+        sib_send[o, at, :] = term(((xx + o) & (nx - 1)) * 2 + 1 - core, h * middle, middle).astype(BF16)
+        sib_copy(o, h).start()
+
+    def combined(o, h):
+        own_term = term(((xx + o) & (nx - 1)) * 2 + core, h * middle, middle)
+        sib_copy(o, h).wait_recv()
+        return own_term + sib_recv[o, h * middle : (h + 1) * middle, :].astype(F32)
 
     def part_copy(slot, o, low, size, sign):
         return pltpu.make_async_remote_copy(
@@ -538,7 +578,7 @@
             device_id_type=MESH,
         )
 
-    middle = rows // 2
+    top, low_half = slice(0, middle), slice(middle, rows)
     parts_sent = []
     if nx == 4:
         far_up = part_copy(0, 2, 0, middle, 1)
@@ -548,70 +588,59 @@
         down_plain = part_copy(4, 3, 0, middle, -1)
         down_added = part_copy(5, 3, middle, middle, -1)
         parts_sent = [far_up, far_down, up_plain, up_added, down_plain, down_added]
-        to_sibling(2)
-        to_sibling(1)
-        x_send[2] = combined(2).astype(BF16)
+        for o, h in ((2, 0), (2, 1), (1, 1), (3, 0)):
+            to_sibling(o, h)
+        x_send[2, top, :] = combined(2, 0).astype(BF16)
         far_up.start()
+        x_send[2, low_half, :] = combined(2, 1).astype(BF16)
         far_down.start()
-        to_sibling(3)
-        up = combined(1)
-        x_send[1, middle:, :] = up[middle:].astype(BF16)
+        to_sibling(1, 0)
+        to_sibling(3, 1)
+        x_send[1, low_half, :] = combined(1, 1).astype(BF16)
         up_plain.start()
-        to_sibling(0)
-        down = combined(3)
-        x_send[3, :middle, :] = down[:middle].astype(BF16)
+        x_send[3, top, :] = combined(3, 0).astype(BF16)
         down_plain.start()
+        to_sibling(0, 0)
+        to_sibling(0, 1)
+        up = combined(1, 0)
+        down = combined(3, 1)
         far_up.wait_recv()
-        x_send[1, :middle, :] = (up[:middle] + x_recv[2, :middle, :].astype(F32)).astype(BF16)
+        x_send[1, top, :] = (up + x_recv[2, top, :].astype(F32)).astype(BF16)
         up_added.start()
         far_down.wait_recv()
-        x_send[3, middle:, :] = (down[middle:] + x_recv[2, middle:, :].astype(F32)).astype(BF16)
+        x_send[3, low_half, :] = (down + x_recv[2, low_half, :].astype(F32)).astype(BF16)
         down_added.start()
-        result = combined(0)
-        for copy in (up_plain, down_plain, up_added, down_added):
-            copy.wait_recv()
-        result = result + x_recv[1].astype(F32) + x_recv[3].astype(F32)
+        first, second = combined(0, 0), combined(0, 1)
+        down_plain.wait_recv()
+        first = first + x_recv[3, top, :].astype(F32)
+        up_plain.wait_recv()
+        second = second + x_recv[1, low_half, :].astype(F32)
+        up_added.wait_recv()
+        out_ref[top, :] = (first + x_recv[1, top, :].astype(F32)).astype(BF16)
+        down_added.wait_recv()
+        out_ref[low_half, :] = (second + x_recv[3, low_half, :].astype(F32)).astype(BF16)
     else:
-        turns = [o for o in (1, 0) if o < nx]
-        to_sibling(turns[0])
-        for k, o in enumerate(turns):
-            if k + 1 < len(turns):
-                to_sibling(turns[k + 1])
-            result = combined(o)
-            if o:
-                x_send[o] = result.astype(BF16)
-                whole = part_copy(0, 1, 0, rows, 1)
-                whole.start()
-                parts_sent += [whole]
-        for copy in parts_sent:
-            copy.wait_recv()
-            result = result + x_recv[1].astype(F32)
-    out_ref[...] = result.astype(out_ref.dtype)
-
-    for kind in order:
-        for sign in (1, -1):
-            for hop in range(1, half + 1):
-                if exists(sign, kind, hop):
-                    z_copy(sign, kind, hop, True).wait_send()
-    y_copy("a", 1, 0, True).wait_send()
-    for hop in range(half + 1):
-        for sign in (1, -1):
-            if (hop == 0 or hop == half) and sign == -1:
-                continue
-            y_copy("b", sign, hop, True).wait_send()
-
-    @pl.when(decoder)
-    def _():
-        for o in range(1, 2 * nx):
-            cot_copy(mp, o, sibling).wait_send()
+        for o in range(nx):
+            for h in range(2):
+                to_sibling(o, h)
+        if nx == 2:
+            whole = part_copy(0, 1, 0, rows, 1)
+            parts_sent += [whole]
+            x_send[1, top, :] = combined(1, 0).astype(BF16)
+            x_send[1, low_half, :] = combined(1, 1).astype(BF16)
+            whole.start()
+            whole.wait_recv()
+        for h, at in enumerate((top, low_half)):
+            result = combined(0, h)
+            if nx == 2:
+                result = result + x_recv[1, at, :].astype(F32)
+            out_ref[at, :] = result.astype(BF16)
 
     for part in range(2):
-        wait_bytes(hop_send.at[part], send1.at[part], n_dp - 1)
         wait_bytes(hop_send.at[2 + part], send2.at[part], n_dp)
-    for o in range(nx):
-        sib_copy(o).wait_send()
-    for copy in parts_sent:
-        copy.wait_send()
+    wait_bytes(c_send.at[0], sib_send, nx)
+    if nx > 1:
+        wait_bytes(c_send.at[1], x_send, nx - 1)
 
 
 def shards(n_dp, n_mp, layer_rows, cotangent, norm_gains, projections, enc_len, dec_len, enc_dev, dec_dev):
@@ -651,7 +680,7 @@
             pltpu.VMEM((rows, LANES), F32),
             pltpu.VMEM((8, far_rows), F32),
             pltpu.VMEM((sides * LANES // HEAD, far_rows, rows), F32),
-            pltpu.VMEM((n_dp * sides * keep, LANES), F32),
+            pltpu.VMEM((rows, rows), BF16),
             pltpu.VMEM((2, n_dp, sides * keep, LANES), BF16),
             pltpu.VMEM((2, n_dp, sides * keep, LANES), BF16),
             pltpu.VMEM((2, n_dp, sides * turns * EX_DEV, LANES), BF16),
@@ -671,7 +700,7 @@
             dma((4,)),
             dma((2,)),
             dma((2,)),
-            dma((nx,)),
+            dma((nx, 2)),
             dma((6,)),
         ],
         compiler_params=pltpu.CompilerParams(

time: 111 us -> 108 us (0.973)
  Pallas kernels: 109 us -> 106 us
    pallas_call x1, Pallas kernels: 109 us -> 106 us  [shards(): pl.pallas_call(functools.partial(kernel, n_dp, n_mp), out_shape=jax.Shape...]
where the time goes in v4:
time: 108 us
  Pallas kernels  106 us (98%)
  local copies, waits for them, and re-layouts  1.67 us (2%)
    pallas_call x1, Pallas kernels, shards(): pl.pallas_call(functools.partial(kernel, n_dp, n_mp), out_shape=jax.Shape...  106 us

profile of v4, /device:TPU:1, one launch (start us, length us, event | category | flops | bytes accessed | tf_op | source)
XLA Modules:
  0.0 107.6 jit_solution(3030993616164120568)
XLA Ops:
  0.0 106.0 %shard_map.82 = bf16[256,512]{1,0:T(8,128)(2,1)} custom-call(bf16[256,4096]{1,0:T(8,128)(2,1)} %bitcast.7, f32[1,4096]{1,0:T(1,128)} %gain_hbm.1, bf16[128,2,256]{2,1,0:T(2,128)(2,1)} %bitcast.9, bf16[256,512]{1,0:T(8,128)(2,1)} %cot_hbm.1, s32[1,256]{1,0:T(1,128)} %bitcast.10, s32[1,256]{1,0:T(1,128)} %bitcast.11, s32[1,256]{1,0:T(1,128)} %bitcast.12, ...), custom_call_target="tpu_custom_call" | custom-call | tf_op jit(solution)/shard_map/pallas_call | solution.py:662
  106.0 1.7 %copy.10 = bf16[1,256,512]{2,1,0:T(8,128)(2,1)} copy(bf16[1,256,512]{2,1,0:T(8,128)(2,1)} %bitcast.8) | data formatting | bytes 524288

commit v5 on v4

--- a/solution.py
+++ b/solution.py
@@ -11,7 +11,8 @@
 EX_DEV = 8
 EPS = 1e-06
 LANES = 128
-CUT = 64
+CUT = 48
+CUT2 = 96
 MESH = pl.DeviceIdType.MESH
 F32 = jnp.float32
 BF16 = jnp.bfloat16
@@ -120,17 +121,15 @@
     wall[own, width:] = w_ref[:, 1, :]
     pl.semaphore_wait(barrier, len(greeted))
 
-    spans = {"b": (CUT, depth - CUT), "a": (0, CUT), "o": (0, CUT)}
-    order = ("b", "a", "o")
+    spans = {"b": (CUT, CUT2 - CUT), "c": (CUT2, depth - CUT2), "a": (0, CUT), "o": (0, CUT)}
+    order = ("b", "c", "a", "o")
 
     def span(kind, y, zb):
         first, size = spans[kind]
         return wall.at[pl.ds(pl.multiple_of((y * nz + zb) * depth + first, 16), size), :]
 
-    def exists(sign, kind, hop):
-        if hop < half:
-            return True
-        return hop == half and ((kind == "b") == (sign == 1))
+    def at_last(sign, kind):
+        return (kind in "bc") == (sign == 1)
 
     def z_copy(sign, kind, hop, sending):
         y = 1 - yl if kind == "o" else yl
@@ -145,29 +144,25 @@
             device_id_type=MESH,
         )
 
-    def y_slot(sign, hop):
-        if hop == 0:
-            return 0
-        return hop if sign == 1 else half + hop
-
-    def y_copy(kind, sign, hop, sending):
-        y = yl if sending else 1 - yl
-        part = span(kind, y, (z - sign * hop) & (nz - 1))
-        slot = nz if kind == "a" else y_slot(sign, hop)
+    def y_copy(kind, zb, slot, sending):
+        piece = span(kind, yl if sending else 1 - yl, zb)
         return pltpu.make_async_remote_copy(
-            src_ref=part,
-            dst_ref=part,
+            src_ref=piece,
+            dst_ref=piece,
             send_sem=w_send_sem,
-            recv_sem=y_sems.at[slot],
+            recv_sem=y_sems.at["bca".index(kind), slot],
             device_id=(section, (1 - yl) * nz + z, mp),
             device_id_type=MESH,
         )
 
-    for kind in ("b", "a"):
+    for kind in ("b", "c", "a"):
         for sign in (1, -1):
-            if exists(sign, kind, 1):
+            if half > 1 or at_last(sign, kind):
                 z_copy(sign, kind, 1, True).start()
-        y_copy("a" if kind == "b" else "b", 1, 0, True).start()
+        if kind == "b":
+            y_copy("a", z, 0, True).start()
+    for kind in "bc":
+        y_copy(kind, z, 0, True).start()
 
     per_mp = features // n_mp // LANES
 
@@ -193,15 +188,15 @@
                 cot_copy(mp, o, ((xx + o) & (nx - 1)) * 2 + core).start()
         cot_copy(mp, nx, sibling).start()
 
-    y_copy("a", 1, 0, False).wait_recv()
+    y_copy("a", z, 0, False).wait_recv()
     for sign in (1, -1):
-        if exists(sign, "o", 1):
+        if half > 1 or at_last(sign, "o"):
             z_copy(sign, "o", 1, True).start()
 
     step = 32 if rows % 32 == 0 else rows
 
-    def norm_rows(i):
-        at = pl.ds(i * step, step)
+    def norm_rows(i, carry):
+        at = pl.ds(pl.multiple_of(i * step, step), step)
         values = x_ref[at, :].astype(F32)
         inverse = lax.rsqrt(jnp.mean(values * values, axis=1, keepdims=True) + EPS)
         inv_ref[at, :] = jnp.broadcast_to(inverse, (step, LANES))
@@ -213,6 +208,8 @@
         def _():
             for c in range(features // LANES):
                 left1[c, at, :] = normed[:, c * LANES : (c + 1) * LANES]
+
+        return carry
 
     count = EX_DEV * n_dp
     far_rows = n_dp * turns * EX_DEV
@@ -325,53 +322,76 @@
         acc[:, :width] += total0
         acc[:, width:] += total1
 
-    def arrived(sign, hop):
-        y_copy("b", sign, hop, False).wait_recv()
-        product(yl, (z - sign * hop) & (nz - 1))
-
-    def cot_pass(o):
-        @pl.when(decoder)
+    def arrived(k, carry):
+        hop, up = (k + 1) // 2, k & 1
+        zb = (z - jnp.where(up == 1, hop, -hop)) & (nz - 1)
+        slot = jnp.where(k == 0, 0, hop + (1 - up) * half)
+        for kind in "bc":
+            y_copy(kind, zb, slot, False).wait_recv()
+        product(yl, zb)
+        return carry
+
+    def cot_pass(now):
+        @pl.when(decoder & now)
         def _():
-            owner = (xx - o + nx) % nx * 2 + core
-            cot_copy(owner, o, sibling).wait_recv()
-            cot_copy(owner, nx + o, sibling).start()
-
-    def cot_wait():
-        @pl.when(decoder)
+            for o in (1, 3, 2):
+                if o < nx:
+                    owner = (xx - o + nx) % nx * 2 + core
+                    cot_copy(owner, o, sibling).wait_recv()
+                    cot_copy(owner, nx + o, sibling).start()
+
+    def cot_wait(now):
+        @pl.when(decoder & now)
         def _():
             for o in range(nx):
                 owner = (xx - o + nx) % nx * 2 + 1 - core
                 cot_copy(owner, nx + o, sibling).wait_recv()
 
-    def first_norm():
-        inputs[2].wait()
-        inputs[3].wait()
-        norm_rows(0)
-
-    acc[...] = jnp.zeros_like(acc)
-    items = [first_norm] + [functools.partial(norm_rows, i) for i in range(1, rows // step)]
-    items += [spread_rows, starts, own_ranks, far_ranks] + [functools.partial(pick_rows, t) for t in range(turns)]
-    items += [functools.partial(pick_side, b, t) for b in range(sides) for t in range(turns)]
-    late = [functools.partial(cot_pass, o) for o in (1, 3, 2) if o < nx] + [cot_wait]
-    late += [functools.partial(arrived, 1, 0)]
-    for hop in range(1, half + 1):
-        if hop == max(1, half - 3):
-            items += late
-            late = []
+    def pass_on(hop, last):
         for kind in order:
             for sign in (1, -1):
-                if exists(sign, kind, hop):
-                    z_copy(sign, kind, hop, False).wait_recv()
-                    if exists(sign, kind, hop + 1):
-                        z_copy(sign, kind, hop + 1, True).start()
-                    if kind == "b":
-                        y_copy("b", sign, hop, True).start()
-                    if items:
-                        items.pop(0)()
-        for sign in (1, -1) if hop < half else (1,):
-            (late if late else items).append(functools.partial(arrived, sign, hop))
-    for item in items:
-        item()
+                if last and not at_last(sign, kind):
+                    continue
+                z_copy(sign, kind, hop, False).wait_recv()
+                if not last:
+                    onward = z_copy(sign, kind, hop + 1, True)
+                    if at_last(sign, kind):
+                        onward.start()
+                    else:
+                        pl.when(hop + 1 < half)(onward.start)
+                if kind in "bc":
+                    slot = hop if sign == 1 else half + hop
+                    y_copy(kind, (z - sign * hop) & (nz - 1), slot, True).start()
+
+    acc[...] = jnp.zeros_like(acc)
+    spread_rows()
+    inputs[2].wait()
+    inputs[3].wait()
+    norm_hops = max(1, min(4, half - 1))
+    chunks = rows // step
+    share_of = -(-chunks // norm_hops)
+
+    def one_hop(hop, carry):
+        pass_on(hop, False)
+        low = jnp.minimum((hop - 1) * share_of, chunks)
+        lax.fori_loop(low, jnp.minimum(low + share_of, chunks), norm_rows, 0)
+        cot_pass(hop == norm_hops)
+        cot_wait(hop == norm_hops + 1)
+        high = jnp.where(hop > norm_hops, 2 * hop - 1, 0)
+        low = jnp.where(hop > norm_hops + 1, 2 * hop - 3, 0)
+        lax.fori_loop(low, high, arrived, 0)
+        return carry
+
+    lax.fori_loop(1, half, one_hop, 0)
+    if half == 1:
+        lax.fori_loop(0, chunks, norm_rows, 0)
+        cot_pass(True)
+    pass_on(half, True)
+    if half - 1 > norm_hops:
+        lax.fori_loop(2 * half - 3, 2 * half, arrived, 0)
+    else:
+        cot_wait(True)
+        lax.fori_loop(0, 2 * half, arrived, 0)
 
     pl.semaphore_signal(cross_sem, inc=1, device_id=(across, dp, mp), device_id_type=MESH)
 
@@ -418,6 +438,14 @@
 
         to_all(send_to)
         send_to((1 - yl) * nz + z)
+
+    starts()
+    own_ranks()
+    far_ranks()
+    for turn in range(turns):
+        pick_rows(turn)
+        for b in range(sides):
+            pick_side(b, turn)
 
     for part in range(2):
         local_copy(part).wait()
@@ -691,8 +719,8 @@
             pltpu.VMEM((nx, rows, columns), BF16),
             dma((4,)),
             pltpu.SemaphoreType.REGULAR,
-            dma((2, 3, max(1, nz // 2))),
-            dma((nz + 1,)),
+            dma((2, 4, max(1, nz // 2))),
+            dma((3, nz)),
             dma((2 * nx,)),
             dma,
             dma,

time: 108 us -> 106 us (0.981)
  Pallas kernels: 106 us -> 104 us
    pallas_call x1, Pallas kernels: 106 us -> 104 us  [shards(): pl.pallas_call(functools.partial(kernel, n_dp, n_mp), out_shape=jax.Shape...]
where the time goes in v5:
time: 106 us; the launch traced here: 105 us
  Pallas kernels  104 us (98%)
  local copies, waits for them, and re-layouts  1.67 us (2%)
    pallas_call x1, Pallas kernels, shards(): pl.pallas_call(functools.partial(kernel, n_dp, n_mp), out_shape=jax.Shape...  104 us

profile of v5, /device:TPU:1, one launch (start us, length us, event | category | flops | bytes accessed | tf_op | source)
XLA Modules:
  0.0 105.4 jit_solution(4949217790526189005)
XLA Ops:
  0.0 103.7 %shard_map.82 = bf16[256,512]{1,0:T(8,128)(2,1)} custom-call(bf16[256,4096]{1,0:T(8,128)(2,1)} %bitcast.7, f32[1,4096]{1,0:T(1,128)} %gain_hbm.1, bf16[128,2,256]{2,1,0:T(2,128)(2,1)} %bitcast.9, bf16[256,512]{1,0:T(8,128)(2,1)} %cot_hbm.1, s32[1,256]{1,0:T(1,128)} %bitcast.10, s32[1,256]{1,0:T(1,128)} %bitcast.11, s32[1,256]{1,0:T(1,128)} %bitcast.12, ...), custom_call_target="tpu_custom_call" | custom-call | tf_op jit(solution)/shard_map/pallas_call | solution.py:690
  103.7 1.7 %copy.10 = bf16[1,256,512]{2,1,0:T(8,128)(2,1)} copy(bf16[1,256,512]{2,1,0:T(8,128)(2,1)} %bitcast.8) | data formatting | bytes 524288

commit v6 on v5

--- a/solution.py
+++ b/solution.py
@@ -347,8 +347,8 @@
                 owner = (xx - o + nx) % nx * 2 + 1 - core
                 cot_copy(owner, nx + o, sibling).wait_recv()
 
-    def pass_on(hop, last):
-        for kind in order:
+    def pass_on(hop, last, kinds=order):
+        for kind in kinds:
             for sign in (1, -1):
                 if last and not at_last(sign, kind):
                     continue
@@ -370,16 +370,28 @@
     norm_hops = max(1, min(4, half - 1))
     chunks = rows // step
     share_of = -(-chunks // norm_hops)
+    quota = 5
+
+    def some_work(hop, slot):
+        first = jnp.minimum((hop - 1) * share_of, chunks)
+        middle = jnp.minimum(first + share_of // 2, chunks)
+        end = jnp.minimum(first + share_of, chunks)
+        bounds = (first, middle, end)
+        lax.fori_loop(bounds[slot], bounds[slot + 1], norm_rows, 0)
+        first = (hop - norm_hops - 1) * quota
+        bounds = (first, first + 3, jnp.minimum(first + quota, 2 * hop - 1))
+        late = hop > norm_hops
+        low = jnp.where(late, bounds[slot], 0)
+        high = jnp.where(late, jnp.minimum(bounds[slot + 1], 2 * hop - 1), 0)
+        lax.fori_loop(low, high, arrived, 0)
 
     def one_hop(hop, carry):
-        pass_on(hop, False)
-        low = jnp.minimum((hop - 1) * share_of, chunks)
-        lax.fori_loop(low, jnp.minimum(low + share_of, chunks), norm_rows, 0)
+        pass_on(hop, False, order[:2])
         cot_pass(hop == norm_hops)
         cot_wait(hop == norm_hops + 1)
-        high = jnp.where(hop > norm_hops, 2 * hop - 1, 0)
-        low = jnp.where(hop > norm_hops + 1, 2 * hop - 3, 0)
-        lax.fori_loop(low, high, arrived, 0)
+        some_work(hop, 0)
+        pass_on(hop, False, order[2:])
+        some_work(hop, 1)
         return carry
 
     lax.fori_loop(1, half, one_hop, 0)
@@ -388,7 +400,8 @@
         cot_pass(True)
     pass_on(half, True)
     if half - 1 > norm_hops:
-        lax.fori_loop(2 * half - 3, 2 * half, arrived, 0)
+        done = min((half - 1 - norm_hops) * quota, 2 * half - 3)
+        lax.fori_loop(done, 2 * half, arrived, 0)
     else:
         cot_wait(True)
         lax.fori_loop(0, 2 * half, arrived, 0)

time: 106 us -> 104 us (0.981)
  Pallas kernels: 104 us -> 102 us
    pallas_call x1, Pallas kernels: 104 us -> 102 us  [shards(): pl.pallas_call(functools.partial(kernel, n_dp, n_mp), out_shape=jax.Shape...]
where the time goes in v6:
time: 104 us
  Pallas kernels  102 us (98%)
  local copies, waits for them, and re-layouts  1.67 us (2%)
    pallas_call x1, Pallas kernels, shards(): pl.pallas_call(functools.partial(kernel, n_dp, n_mp), out_shape=jax.Shape...  102 us

profile of v6, /device:TPU:1, one launch (start us, length us, event | category | flops | bytes accessed | tf_op | source)
XLA Modules:
  0.0 103.6 jit_solution(12117997684010033181)
XLA Ops:
  0.0 102.0 %shard_map.82 = bf16[256,512]{1,0:T(8,128)(2,1)} custom-call(bf16[256,4096]{1,0:T(8,128)(2,1)} %bitcast.7, f32[1,4096]{1,0:T(1,128)} %gain_hbm.1, bf16[128,2,256]{2,1,0:T(2,128)(2,1)} %bitcast.9, bf16[256,512]{1,0:T(8,128)(2,1)} %cot_hbm.1, s32[1,256]{1,0:T(1,128)} %bitcast.10, s32[1,256]{1,0:T(1,128)} %bitcast.11, s32[1,256]{1,0:T(1,128)} %bitcast.12, ...), custom_call_target="tpu_custom_call" | custom-call | tf_op jit(solution)/shard_map/pallas_call | solution.py:703
  102.0 1.7 %copy.10 = bf16[1,256,512]{2,1,0:T(8,128)(2,1)} copy(bf16[1,256,512]{2,1,0:T(8,128)(2,1)} %bitcast.8) | data formatting | bytes 524288

commit v7 on v6

--- a/solution.py
+++ b/solution.py
@@ -494,7 +494,7 @@
 
     def softmax(q, k, mask):
         weight = jnp.where(mask, jnp.exp(nt(q, k) * scale), 0.0)
-        return weight * (1.0 / jnp.sum(weight, axis=1, keepdims=True))
+        return weight / jnp.sum(weight, axis=1, keepdims=True)
 
     def backward(probs, dout_s, v):
         probs_bf = probs.astype(BF16)

time: 104 us -> 104 us (level)
  no operation moved by 1% of the time
where the time goes in v7:
time: 104 us
  Pallas kernels  102 us (98%)
  local copies, waits for them, and re-layouts  1.67 us (2%)
    pallas_call x1, Pallas kernels, shards(): pl.pallas_call(functools.partial(kernel, n_dp, n_mp), out_shape=jax.Shape...  102 us

profile of v7, /device:TPU:1, one launch (start us, length us, event | category | flops | bytes accessed | tf_op | source)
XLA Modules:
  0.0 103.6 jit_solution(12117997684010033181)
XLA Ops:
  0.0 102.0 %shard_map.82 = bf16[256,512]{1,0:T(8,128)(2,1)} custom-call(bf16[256,4096]{1,0:T(8,128)(2,1)} %bitcast.7, f32[1,4096]{1,0:T(1,128)} %gain_hbm.1, bf16[128,2,256]{2,1,0:T(2,128)(2,1)} %bitcast.9, bf16[256,512]{1,0:T(8,128)(2,1)} %cot_hbm.1, s32[1,256]{1,0:T(1,128)} %bitcast.10, s32[1,256]{1,0:T(1,128)} %bitcast.11, s32[1,256]{1,0:T(1,128)} %bitcast.12, ...), custom_call_target="tpu_custom_call" | custom-call | tf_op jit(solution)/shard_map/pallas_call | solution.py:703
  102.0 1.7 %copy.10 = bf16[1,256,512]{2,1,0:T(8,128)(2,1)} copy(bf16[1,256,512]{2,1,0:T(8,128)(2,1)} %bitcast.8) | data formatting | bytes 524288
